TPU v7x, 32 devices: a whole 2x2x4 slice. The times are simulated.
32 devices in a mesh: rep: 2 (over y), fsdp: 4 (over x, core), patch: 4 (over z).
Axes of the slice: x: 2, y: 2, z: 4, core: 2. Of those that a mesh axis runs over, the one named last changes fastest.
Arguments:
- latent: bfloat16 [4, 512, 6144], P('rep', 'fsdp', 'patch'), parts along dimension 0, may hold values from -3 to 3
- timestep: int32 [4], P('rep'), parts along dimension 0, may hold values from 0 to 49, as said below
- positions: int32 [1024], P(('rep', 'fsdp')), parts along dimension 0, may hold values from 0 to 511, each once
- modulation: bfloat16 [50, 3, 6144], P(None, None, 'patch'), may hold values from -3 to 3
- qkv_weight: bfloat16 [6144, 3, 3072], P('fsdp', None, 'patch'), may hold values from -0.078125 to 0.078125
- out_weight: bfloat16 [3072, 6144], P('patch', 'fsdp'), may hold values from -1.25 to 1.25
- query_gain: float32 [128], replicated, may hold values from 0.1 to 1.9
- key_gain: float32 [128], replicated, may hold values from 0.1 to 1.9
- stale_keys: bfloat16 [4, 512, 3072], P('rep', 'fsdp', 'patch'), parts along dimension 0, may hold values from -140 to 140
- stale_values: bfloat16 [4, 512, 3072], P('rep', 'fsdp', 'patch'), parts along dimension 0, may hold values from -6 to 6
Outputs:
- block_out: bfloat16 [4, 512, 6144], P('rep', 'fsdp', 'patch'), parts along dimension 0
- new_keys: bfloat16 [4, 512, 3072], P('rep', 'fsdp', 'patch'), parts along dimension 0
- new_values: bfloat16 [4, 512, 3072], P('rep', 'fsdp', 'patch'), parts along dimension 0
There are 2 independent parts, one for each index of `rep`. A program takes and returns all parts, laid end to end along the dimension named above; an argument that names none is the same for every part. Nothing has to cross between parts.
Inputs may be any that keep to these rules, and one draw needn't show every extreme that they name: Each of the 512 grid positions appears once. `timestep`: the 2 entries are distinct.
All inputs are finite; a program needn't handle non-finite values.
Results may differ from a plain program's by a relative error of at most 0.012.
The roundings to bfloat16 on the way count: a program that leaves them out, or rounds other values in their place, can miss the bound.
Values may be sent and summed in bfloat16 or wider, within the bound.
No kernel may reach another device: no remote copies, remote signals or barrier semaphores. Data moves between devices by JAX's collectives and lax.ppermute only.
A program may use at most 128 MiB of HBM per device.

v0:
```python
import jax
import jax.numpy as jnp
from jax import lax
from jax.sharding import PartitionSpec as P

GRID_W = 62


EPS = 1e-06


def norm_heads(values, gain):
    return values * lax.rsqrt(jnp.mean(values * values, axis=-1, keepdims=True) + EPS) * gain


def rotate(values, places):
    quarter = values.shape[-1] // 4
    freq = 10000.0 ** (-jnp.arange(quarter, dtype=jnp.float32) / quarter)
    row_pos = (places // GRID_W).astype(jnp.float32)
    col_pos = (places % GRID_W).astype(jnp.float32)
    pieces = []
    for coords, lower in ((row_pos, 0), (col_pos, 2 * quarter)):
        angle = coords[:, None] * freq[None, :]
        cosine = jnp.cos(angle)[None, :, None, :]
        sine = jnp.sin(angle)[None, :, None, :]
        first = values[..., lower : lower + quarter]
        second = values[..., lower + quarter : lower + 2 * quarter]
        pieces.append(first * cosine - second * sine)
        pieces.append(second * cosine + first * sine)
    return jnp.concatenate(pieces, axis=-1)


def shards(
    latent,
    timestep,
    positions,
    modulation,
    qkv_weight,
    out_weight,
    query_gain,
    key_gain,
    stale_keys,
    stale_values,
):
    samples, rows, part_width = latent.shape
    head_size = query_gain.shape[0]
    local_width = qkv_weight.shape[2]
    heads = local_width // head_size
    mine = lax.axis_index("fsdp")
    factor = 1.0 / head_size**0.5
    levels = modulation.shape[0]
    onehot = (timestep[:, None] == jnp.arange(levels, dtype=jnp.int32)[None, :]).astype(
        jnp.bfloat16
    )
    picked = jnp.einsum(
        "st,tcf->scf", onehot, modulation, preferred_element_type=jnp.float32
    ).astype(jnp.bfloat16)
    gate = picked[:, 2, :].astype(jnp.float32)[:, None, :]
    whole, mod_whole = (
        lax.all_gather(latent, "patch", axis=2, tiled=True),
        lax.all_gather(picked, "patch", axis=2, tiled=True),
    )
    values = whole.astype(jnp.float32)
    mean = jnp.mean(values, axis=-1, keepdims=True)
    centered = values - mean
    spread = jnp.mean(centered * centered, axis=-1, keepdims=True)
    shift = mod_whole[:, 0].astype(jnp.float32)[:, None, :]
    scale = mod_whole[:, 1].astype(jnp.float32)[:, None, :]
    modded = (centered * lax.rsqrt(spread + EPS) * (1.0 + scale) + shift).astype(jnp.bfloat16)
    projected = jnp.einsum(
        "std,dch->stch",
        modded,
        lax.all_gather(qkv_weight, "fsdp", axis=0, tiled=True),
        preferred_element_type=jnp.float32,
    )
    queries = rotate(
        norm_heads(projected[:, :, 0].reshape(samples, rows, heads, head_size), query_gain),
        positions,
    ).astype(jnp.bfloat16)
    fresh_keys = rotate(
        norm_heads(projected[:, :, 1].reshape(samples, rows, heads, head_size), key_gain), positions
    ).astype(jnp.bfloat16)
    fresh_flat = projected[:, :, 2].astype(jnp.bfloat16)
    fresh_values = fresh_flat.reshape(samples, rows, heads, head_size)
    scores = (
        jnp.einsum("sqhd,skhd->shqk", queries, fresh_keys, preferred_element_type=jnp.float32)
        * factor
    )
    top = jnp.max(scores, axis=-1)
    weights = jnp.exp(scores - top[..., None])
    total = jnp.sum(weights, axis=-1)
    summed = jnp.einsum(
        "shqk,skhd->shqd",
        weights.astype(jnp.bfloat16),
        fresh_values,
        preferred_element_type=jnp.float32,
    )
    own_low = mine * rows
    run_total = total
    run_sum = summed
    key_piece = lax.all_gather(stale_keys, "fsdp", axis=1, tiled=True).reshape(
        samples, -1, heads, head_size
    )
    value_piece = lax.all_gather(stale_values, "fsdp", axis=1, tiled=True).reshape(
        samples, -1, heads, head_size
    )
    count = key_piece.shape[1]
    piece_scores = (
        jnp.einsum("sqhd,skhd->shqk", queries, key_piece, preferred_element_type=jnp.float32)
        * factor
    )
    index = jnp.arange(count, dtype=jnp.int32)
    skipped = (index >= own_low) & (index < own_low + rows)
    piece_scores = jnp.where(skipped[None, None, None, :], -1e30, piece_scores)
    new_top = jnp.maximum(top, jnp.max(piece_scores, axis=-1))
    piece_weights = jnp.exp(piece_scores - new_top[..., None])
    fade = jnp.exp(top - new_top)
    run_total = run_total * fade + jnp.sum(piece_weights, axis=-1)
    run_sum = run_sum * fade[..., None] + jnp.einsum(
        "shqk,skhd->shqd",
        piece_weights.astype(jnp.bfloat16),
        value_piece,
        preferred_element_type=jnp.float32,
    )
    mixed = (
        (run_sum / run_total[..., None])
        .transpose(0, 2, 1, 3)
        .reshape(samples, rows, local_width)
        .astype(jnp.bfloat16)
    )
    terms = jnp.einsum(
        "sth,hn->stn",
        mixed,
        lax.all_gather(out_weight, "fsdp", axis=1, tiled=True),
        preferred_element_type=jnp.float32,
    )
    attended = lax.psum_scatter(
        terms.astype(jnp.bfloat16), "patch", scatter_dimension=2, tiled=True
    ).astype(jnp.float32)
    block_out = (latent.astype(jnp.float32) + gate * attended).astype(jnp.bfloat16)
    return (block_out, fresh_keys.reshape(samples, rows, local_width), fresh_flat)


def solution(mesh):
    in_specs = (
        P("rep", "fsdp", "patch"),
        P("rep"),
        P(("rep", "fsdp")),
        P(None, None, "patch"),
        P("fsdp", None, "patch"),
        P("patch", "fsdp"),
        P(),
        P(),
        P("rep", "fsdp", "patch"),
        P("rep", "fsdp", "patch"),
    )
    out_specs = (P("rep", "fsdp", "patch"), P("rep", "fsdp", "patch"), P("rep", "fsdp", "patch"))
    return jax.shard_map(shards, mesh=mesh, in_specs=in_specs, out_specs=out_specs, check_vma=False)
```

profile of v0, /device:TPU:0, one launch (start us, length us, event | category | flops | bytes accessed | tf_op | source)
XLA Modules:
  0.0 434.0 jit_solution(2539902188661399968)
XLA Ops:
  7.2 0.7 all-gather.12.cloned.1.call-update
  8.0 0.7 all-gather.6.cloned.1.call-update
  9.7 0.9 copy.25
  11.5 14.9 %all_gather.19 = bf16[2,3,6144]{2,0,1:T(2,128)(2,1)S(1)} all-gather(bf16[2,3,1536]{2,0,1:T(2,128)(2,1)S(1)} %convolution_convert_fusion), channel_id=1, replica_groups=mesh['rep'=2,'fsdp'=4,'patch'=4] {'patch'}, dimensions={2}, use_global_device_ids=true | all-gather | bytes 92160 | tf_op jit(solution)/shard_map/all_gather | solution.py:61
  27.0 4.9 %all-gather.12.cloned.1.call-done = bf16[2,512,768]{2,1,0:T(8,128)(2,1)} async-done(((bf16[2,128,768]{2,1,0:T(8,128)(2,1)}), bf16[2,512,768]{2,1,0:T(8,128)(2,1)}) %all-gather.12.cloned.1.call-update) | async-done | bytes 1572880 | tf_op jit(solution)/shard_map/all_gather | solution.py:104
  32.0 2.6 copy.27
  34.6 62.5 %all-gather.6.cloned.1.call-done = bf16[2,128,6144]{2,1,0:T(8,128)(2,1)} async-done(((bf16[2,128,1536]{2,1,0:T(8,128)(2,1)}), bf16[2,128,6144]{2,1,0:T(8,128)(2,1)}) %all-gather.6.cloned.1.call-update) | async-done | bytes 3145744 | tf_op jit(solution)/shard_map/all_gather | solution.py:60
  97.0 2.5 convert_reduce_fusion
  99.9 1.0 fusion.9
  100.9 168.3 %all-gather.8.cloned.1.call-done = bf16[6144,3,768]{2,0,1:T(8,128)(2,1)} async-done(((bf16[1536,3,768]{2,0,1:T(8,128)(2,1)}), bf16[6144,3,768]{2,0,1:T(8,128)(2,1)}) %all-gather.8.cloned.1.call-update) | async-done | bytes 28311568 | tf_op jit(solution)/shard_map/all_gather | solution.py:73
  269.1 14.9 %fusion = f32[2,128,3,768]{3,1,2,0:T(8,128)S(1)} fusion(bf16[6144,3,768]{2,0,1:T(8,128)(2,1)} %all-gather.8.cloned.1.call-done, bf16[2,128,6144]{2,1,0:T(8,128)(2,1)} %all-gather.6.cloned.1.call-done, f32[2,6144]{1,0:T(2,128)S(1)} %fusion.39, f32[2,6144]{1,0:T(2,128)S(1)} %add_bitcast_fusion, f32[2,128]{1,0:T(2,128)S(1)} %add_rsqrt_fusion.2, ...), kind=kOutput, calls=%fused_computation | convolution fusion | flops 7257194496 | bytes 33916928 | tf_op jit(solution)/shard_map/std,dch->stch/dot_general | solution.py:70
  284.2 1.3 copy-done.4
  285.8 1.1 copy.22
  287.5 0.9 copy.23
  288.5 1.4 multiply_multiply_fusion
  293.1 2.1 fusion.19
  295.4 1.0 fusion.20
  296.6 0.9 fusion.28
  297.9 58.8 %all-gather.14.cloned.1.call-done = bf16[768,6144]{1,0:T(8,128)(2,1)} async-done(((bf16[768,1536]{1,0:T(8,128)(2,1)}), bf16[768,6144]{1,0:T(8,128)(2,1)}) %all-gather.14.cloned.1.call-update) | async-done | bytes 9437200 | tf_op jit(solution)/shard_map/all_gather | solution.py:134
  356.7 7.7 %fusion.4 = bf16[2,128,6144]{2,1,0:T(8,128)(2,1)} fusion(bf16[2,128,768]{1,2,0:T(8,128)(2,1)S(1)} %bitcast.76, bf16[768,6144]{1,0:T(8,128)(2,1)} %all-gather.14.cloned.1.call-done), kind=kOutput, calls=%fused_computation.6 | convolution fusion | flops 2417491968 | bytes 12976128 | tf_op jit(solution)/shard_map/sth,hn->stn/dot_general | solution.py:131
  364.7 0.9 copy.30
  365.6 1.9 slice_bitcast_fusion.2
  367.6 57.3 %reduce-scatter.2.cloned.1.call-done = bf16[2,128,1536]{2,1,0:T(8,128)(2,1)} async-done(((bf16[2,128,6144]{2,1,0:T(8,128)(2,1)}), bf16[2,128,1536]{2,1,0:T(8,128)(2,1)}) %reduce-scatter.2.cloned.1.call-update) | async-done | bytes 786448 | tf_op jit(solution)/shard_map/reduce_scatter | solution.py:137
  424.8 2.3 add_convert_fusion
  (64 shorter events, 8.0 us)
Async XLA Ops:
  7.2 4.1 copy-start
  7.2 24.8 %all-gather.12.cloned.1.call-start = ((), (), s32[]{:S(2)}) async-start(), calls=%async_computation.4 | async-start | bytes 1966080 | tf_op jit(solution)/shard_map/all_gather | solution.py:104
  7.9 89.1 %all-gather.6.cloned.1.call-start = ((), (), s32[]{:S(2)}) async-start(), calls=%async_computation.1 | async-start | bytes 3932160 | tf_op jit(solution)/shard_map/all_gather | solution.py:60
  8.7 1.0 copy-start.6
  8.7 260.4 %all-gather.8.cloned.1.call-start = ((), (), s32[]{:S(2)}) async-start(), calls=%async_computation.2 | async-start | bytes 35389440 | tf_op jit(solution)/shard_map/all_gather | solution.py:73
  9.4 1.8 copy-start.8
  9.4 17.0 %copy-start.11 = (s32[128]{0:T(128)S(1)}, s32[128]{0:T(128)}, u32[]{:S(2)}) copy-start(s32[128]{0:T(128)} %param.12) | copy-start | bytes 1540
  9.4 283.7 %all-gather.10.cloned.1.call-start = ((), (), s32[]{:S(2)}) async-start(), calls=%async_computation.3 | async-start | bytes 1966080 | tf_op jit(solution)/shard_map/all_gather | solution.py:101
  10.6 346.1 %all-gather.14.cloned.1.call-start = ((), (), s32[]{:S(2)}) async-start(), calls=%async_computation.5 | async-start | bytes 11796480 | tf_op jit(solution)/shard_map/all_gather | solution.py:134
  11.2 413.6 %reduce-scatter.2.cloned.1.call-start = ((), (), s32[]{:S(2)}) async-start(), calls=%async_computation.6 | async-start | bytes 3932160 | tf_op jit(solution)/shard_map/reduce_scatter | solution.py:137
  97.0 2.8 copy-start.2
  284.0 1.5 copy-start.4
  285.8 2.7 copy-start.9
  289.9 1.3 copy-start.10
  295.2 1.4 copy-start.5
  296.3 1.2 copy-start.7
  364.4 60.4 %copy-start.3 = (bf16[2,128,1536]{2,1,0:T(8,128)(2,1)S(1)}, bf16[2,128,1536]{2,1,0:T(8,128)(2,1)}, u32[]{:S(2)}) copy-start(bf16[2,128,1536]{2,1,0:T(8,128)(2,1)} %param.10) | copy-start | bytes 2359300
  364.4 62.7 %copy-start.1 = (bf16[50,3,1536]{2,0,1:T(8,128)(2,1)S(1)}, bf16[50,3,1536]{2,0,1:T(8,128)(2,1)}, u32[]{:S(2)}) copy-start(bf16[50,3,1536]{2,0,1:T(8,128)(2,1)} %param.13) | copy-start | bytes 1382404
Sparse Core Ops, SparseCore 0:
  9.6 22.3 all-gather.11
  33.5 63.4 all-gather.5
  98.6 170.4 all-gather.7
  271.1 19.8 all-gather.9
  292.4 64.2 all-gather.13
  364.6 60.2 reduce-scatter.1
where the time goes:
time: 434 us
  waiting for transfers between devices  354 us (82%)
  matrix products  26.6 us (6%)
  blocking collectives  14.9 us (3%)
  between operations  14.4 us (3%)
  other arithmetic  11.8 us (3%)
  local copies, waits for them, and re-layouts  11.7 us (3%)
    all_gather x1, waiting for transfers between devices, shards(): lax.all_gather(qkv_weight, 'fsdp', axis=0, tiled=True)  168 us
    all_gather x1, waiting for transfers between devices, shards(): lax.all_gather(latent, 'patch', axis=2, tiled=True)  62.5 us
    all_gather x1, waiting for transfers between devices, shards(): lax.all_gather(out_weight, 'fsdp', axis=1, tiled=True)  58.8 us
    reduce_scatter x1, waiting for transfers between devices, shards(): lax.psum_scatter(terms.astype(jnp.bfloat16), 'patch', scatter_dimension=2...  57.3 us
    dot_general x1, matrix products, shards(): jnp.einsum('std,dch->stch', modded, lax.all_gather(qkv_weight, 'fsdp', ax...  14.9 us
    all_gather x1, blocking collectives, shards(): lax.all_gather(picked, 'patch', axis=2, tiled=True)  14.9 us
  transfers between devices with their start and end apart: 6, of which 5 were waited for; matrix products, arithmetic and copies ran while one was open for 9% of the time, Pallas kernels for 0%

commit v1 on v0

--- a/solution.py
+++ b/solution.py
@@ -1,6 +1,10 @@
+import functools
+
 import jax
 import jax.numpy as jnp
 from jax import lax
+from jax.experimental import pallas as pl
+from jax.experimental.pallas import tpu as pltpu
 from jax.sharding import PartitionSpec as P
 
 GRID_W = 62
@@ -30,7 +34,17 @@
     return jnp.concatenate(pieces, axis=-1)
 
 
-def shards(
+def pick_rows(timestep, modulation):
+    levels = modulation.shape[0]
+    onehot = (timestep[:, None] == jnp.arange(levels, dtype=jnp.int32)[None, :]).astype(
+        jnp.bfloat16
+    )
+    return jnp.einsum(
+        "st,tcf->scf", onehot, modulation, preferred_element_type=jnp.float32
+    ).astype(jnp.bfloat16)
+
+
+def shards_any(
     latent,
     timestep,
     positions,
@@ -48,13 +62,7 @@
     heads = local_width // head_size
     mine = lax.axis_index("fsdp")
     factor = 1.0 / head_size**0.5
-    levels = modulation.shape[0]
-    onehot = (timestep[:, None] == jnp.arange(levels, dtype=jnp.int32)[None, :]).astype(
-        jnp.bfloat16
-    )
-    picked = jnp.einsum(
-        "st,tcf->scf", onehot, modulation, preferred_element_type=jnp.float32
-    ).astype(jnp.bfloat16)
+    picked = pick_rows(timestep, modulation)
     gate = picked[:, 2, :].astype(jnp.float32)[:, None, :]
     whole, mod_whole = (
         lax.all_gather(latent, "patch", axis=2, tiled=True),
@@ -141,6 +149,277 @@
     return (block_out, fresh_keys.reshape(samples, rows, local_width), fresh_flat)
 
 
+def norm_kernel(key, own, one, two, three, turns, *rest):
+    outs, held = rest[:4], rest[4]
+    blocks = (own, one, two, three)
+    width = 4 * own.shape[1]
+    mean = sum(jnp.sum(b[...].astype(jnp.float32), axis=-1, keepdims=True) for b in blocks) / width
+    spread = (
+        sum(
+            jnp.sum(jnp.square(b[...].astype(jnp.float32) - mean), axis=-1, keepdims=True)
+            for b in blocks
+        )
+        / width
+    )
+    rate = lax.rsqrt(spread + EPS)
+    for r, block in enumerate(blocks):
+        shift = turns[r, 0:1].astype(jnp.float32)
+        scale = turns[r, 1:2].astype(jnp.float32)
+        centered = block[...].astype(jnp.float32) - mean
+        held[r ^ key[0]] = (centered * rate * (1.0 + scale) + shift).astype(jnp.bfloat16)
+    for j in range(4):
+        outs[j][...] = held[j]
+
+
+def project_kernel(own, pair, over, cross, weight, kept, sent):
+    rows = own.shape[0]
+    every = jnp.concatenate([own[...], over[...], pair[...], cross[...]], axis=0)
+    product = jnp.dot(every, weight[0], preferred_element_type=jnp.float32)
+    for i in range(2):
+        kept[i] = product[i * rows : (i + 1) * rows]
+        sent[i] = product[(i + 2) * rows : (i + 3) * rows]
+
+
+def attend_kernel(
+    at, kept, back, over, s_pair, s_x, s_d, tables, gains,
+    o_own, o_pair, o_x, o_xo, o_d, o_do,
+    keys_out, values_out, near, far, mixed, held,
+):
+    rows, width = keys_out.shape
+    size = gains.shape[1]
+    half = mixed.shape[2]
+    factor = 1.0 / size**0.5
+    lane = lax.broadcasted_iota(jnp.int32, (rows, size), 1)
+    low = (lane // (size // 4)) % 2 == 0
+
+    def summed(first):
+        cols = slice(first, first + size)
+        return kept[0, :, cols] + back[0, :, cols] + over[:, cols].astype(jnp.float32)
+
+    def turned(values, gain):
+        values = values * lax.rsqrt(jnp.mean(values * values, axis=-1, keepdims=True) + EPS) * gain
+        other = jnp.where(
+            low, pltpu.roll(values, size - size // 4, 1), pltpu.roll(values, size // 4, 1)
+        )
+        return (values * tables[0] + other * tables[1]).astype(jnp.bfloat16)
+
+    for h in range(width // size):
+        cols = slice(h * size, (h + 1) * size)
+        query = turned(summed(h * size), gains[0:1])
+        key = turned(summed(width + h * size), gains[1:2])
+        value = summed(2 * width + h * size).astype(jnp.bfloat16)
+        keys_out[:, cols] = key
+        values_out[:, cols] = value
+        keys = jnp.concatenate([key] + [s[0, 0, :, cols] for s in (s_pair, s_x, s_d)], axis=0)
+        seen = jnp.concatenate([value] + [s[1, 0, :, cols] for s in (s_pair, s_x, s_d)], axis=0)
+        scores = (
+            lax.dot_general(
+                query, keys, (((1,), (1,)), ((), ())), preferred_element_type=jnp.float32
+            )
+            * factor
+        )
+        weights = jnp.exp(scores - jnp.max(scores, axis=-1, keepdims=True))
+        total = jnp.sum(weights, axis=-1, keepdims=True)
+        product = jnp.dot(weights.astype(jnp.bfloat16), seen, preferred_element_type=jnp.float32)
+        place = h * size // half
+        start = h * size - place * half
+        mixed[place, :, start : start + size] = (product / total).astype(jnp.bfloat16)
+
+    rep = at[1]
+    for j, (first, second, one, two) in enumerate(
+        (
+            (o_own, o_own, 0, 1),
+            (o_pair, o_pair, 0, 1),
+            (o_x, o_xo, rep, 1 - rep),
+            (o_d, o_do, rep, 1 - rep),
+        )
+    ):
+        top = first[:half] if first.shape[0] == 2 * half else first[...]
+        low_rows = second[half:] if second.shape[0] == 2 * half else second[...]
+        term = jnp.dot(mixed[one], top, preferred_element_type=jnp.float32) + jnp.dot(
+            mixed[two], low_rows, preferred_element_type=jnp.float32
+        )
+        held[j ^ at[0]] = term.astype(jnp.bfloat16)
+    for i in range(2):
+        near[i] = held[2 * i]
+        far[i] = held[2 * i + 1]
+
+
+LIMIT = 56 * 1024 * 1024
+
+
+def params():
+    return pltpu.CompilerParams(vmem_limit_bytes=LIMIT)
+
+
+def run_norm(key, blocks, turns):
+    rows, cols = blocks[0].shape
+    vmem = pl.BlockSpec(memory_space=pltpu.VMEM)
+    shape = jax.ShapeDtypeStruct((rows, cols), jnp.bfloat16)
+    return pl.pallas_call(
+        norm_kernel,
+        in_specs=[pl.BlockSpec(memory_space=pltpu.SMEM)] + [vmem] * 5,
+        out_specs=[vmem] * 4,
+        out_shape=[shape] * 4,
+        scratch_shapes=[pltpu.VMEM((4, rows, cols), jnp.bfloat16)],
+        compiler_params=params(),
+        cost_estimate=pl.CostEstimate(
+            flops=60 * rows * cols, bytes_accessed=16 * rows * cols, transcendentals=0
+        ),
+        name="norm",
+    )(key, *blocks, turns)
+
+
+def run_project(own, pair, over, cross, weight):
+    rows, depth = own.shape
+    wide = weight.shape[2]
+    vmem = pl.BlockSpec((rows, depth), lambda i: (0, 0))
+    out = pl.BlockSpec((2, rows, wide), lambda i: (0, 0, i))
+    shape = jax.ShapeDtypeStruct((2, rows, 3 * wide), jnp.float32)
+    return pl.pallas_call(
+        project_kernel,
+        grid=(3,),
+        in_specs=[vmem] * 4 + [pl.BlockSpec((1, depth, wide), lambda i: (i, 0, 0))],
+        out_specs=[out, out],
+        out_shape=[shape, shape],
+        compiler_params=params(),
+        cost_estimate=pl.CostEstimate(
+            flops=24 * rows * depth * wide,
+            bytes_accessed=6 * depth * wide + 48 * rows * wide,
+            transcendentals=0,
+        ),
+        name="project",
+    )(own, pair, over, cross, weight)
+
+
+def run_attend(s, at, kept, back, over, stale, tables, gains, columns):
+    rows, triple = over.shape
+    width = triple // 3
+    feats = columns[0].shape[1]
+    full = pl.BlockSpec(memory_space=pltpu.VMEM)
+    first = pl.BlockSpec((1, rows, triple), lambda i, at: (0, 0, 0))
+    seen = pl.BlockSpec((2, 1, rows, width), lambda i, at: (0, s, 0, 0))
+    head = jax.ShapeDtypeStruct((rows, width), jnp.bfloat16)
+    term = jax.ShapeDtypeStruct((2, rows, feats), jnp.bfloat16)
+    return pl.pallas_call(
+        attend_kernel,
+        grid_spec=pltpu.PrefetchScalarGridSpec(
+            num_scalar_prefetch=1,
+            grid=(1,),
+            in_specs=[first, first, full] + [seen] * 3 + [full] * 8,
+            out_specs=[full] * 4,
+            scratch_shapes=[
+                pltpu.VMEM((2, rows, width // 2), jnp.bfloat16),
+                pltpu.VMEM((4, rows, feats), jnp.bfloat16),
+            ],
+        ),
+        out_shape=[head, head, term, term],
+        compiler_params=params(),
+        cost_estimate=pl.CostEstimate(
+            flops=8 * rows * width * feats + 16 * rows * rows * width,
+            bytes_accessed=8 * width * feats + 16 * rows * triple,
+            transcendentals=0,
+        ),
+        name="attend",
+    )(at, kept, back, over, *stale, tables, gains, *columns)
+
+
+def shards_four(
+    latent,
+    timestep,
+    positions,
+    modulation,
+    qkv_weight,
+    out_weight,
+    query_gain,
+    key_gain,
+    stale_keys,
+    stale_values,
+):
+    samples, rows, part_width = latent.shape
+    size = query_gain.shape[0]
+    f = lax.axis_index("fsdp")
+    z = lax.axis_index("patch")
+    y = lax.axis_index("rep")
+
+    def to_f(v, d):
+        return lax.ppermute(v, "fsdp", [(i, i ^ d) for i in range(4)])
+
+    def to_y(v):
+        return lax.ppermute(v, "rep", [(0, 1), (1, 0)])
+
+    def to_z(v, d):
+        return lax.ppermute(v, "patch", [(i, i ^ d) for i in range(4)])
+
+    def after(v, *deps):
+        return lax.optimization_barrier((v, *deps))[0]
+
+    stale = jnp.stack([stale_keys, stale_values])
+    s_x = to_f(stale, 2)
+    own = [latent[s] for s in range(samples)]
+    one, two, three = [], [], []
+    for s in range(samples):
+        start = own[s] if s == 0 else after(own[s], one[s - 1], two[s - 1])
+        one.append(to_z(start, 1))
+        two.append(to_z(start, 2))
+        three.append(to_z(after(two[s], s_x), 1))
+
+    picked = pick_rows(timestep, modulation)
+    gate = picked[:, 2, :].astype(jnp.float32)[:, None, :]
+    turn = picked[:, :2]
+    turns = jnp.stack([turn] + [to_z(turn, d) for d in (1, 2, 3)])
+
+    deep = out_weight.shape[0] // 2
+    o_half = lax.dynamic_slice_in_dim(out_weight, y * deep, deep, 0)
+    o_x = to_f(after(o_half, s_x), 2)
+    o_xo = to_y(o_x)
+    columns = (out_weight, to_f(out_weight, 1), o_x, o_xo, to_f(o_x, 1), to_f(o_xo, 1))
+    stale_seen = (to_f(stale, 1), s_x, to_f(s_x, 1))
+
+    quarter = size // 4
+    freq = 10000.0 ** (-jnp.arange(quarter, dtype=jnp.float32) / quarter)
+    row_angle = (positions // GRID_W).astype(jnp.float32)[:, None] * freq
+    col_angle = (positions % GRID_W).astype(jnp.float32)[:, None] * freq
+    row_sin, col_sin = jnp.sin(row_angle), jnp.sin(col_angle)
+    row_cos, col_cos = jnp.cos(row_angle), jnp.cos(col_angle)
+    tables = jnp.stack(
+        [
+            jnp.concatenate([row_cos, row_cos, col_cos, col_cos], axis=-1),
+            jnp.concatenate([-row_sin, row_sin, -col_sin, col_sin], axis=-1),
+        ]
+    )
+    gains = jnp.stack([query_gain, key_gain])
+    key = f ^ z
+    at = jnp.stack([key, y]).astype(jnp.int32)
+
+    weight = qkv_weight.transpose(1, 0, 2)
+    fence = o_x
+    shared = []
+    for s in range(samples):
+        modded = run_norm(at, (own[s], one[s], two[s], three[s]), turns[:, s])
+        over = to_f(after(modded[2], fence), 2)
+        cross = to_f(after(modded[3], fence), 3)
+        fence = over
+        shared.append((modded[0], to_f(modded[1], 1), over, cross))
+    keys, values, outs = [], [], []
+    for s in range(samples):
+        kept, sent = run_project(*shared[s], weight)
+        back = to_f(sent, 1)
+        part = (kept[1] + back[1]).astype(jnp.bfloat16)
+        over = to_f(after(part, o_xo) if s == 0 else part, 2)
+        new_keys, new_values, near, far = run_attend(
+            s, at, kept, back, over, stale_seen, tables, gains, columns
+        )
+        keys.append(new_keys)
+        values.append(new_values)
+        come = to_z(far, 1)
+        pair = near.astype(jnp.float32) + come.astype(jnp.float32)
+        rest = to_z(pair[1].astype(jnp.bfloat16), 2)
+        attended = pair[0] + rest.astype(jnp.float32)
+        outs.append((own[s].astype(jnp.float32) + gate[s] * attended).astype(jnp.bfloat16))
+    return (jnp.stack(outs), jnp.stack(keys), jnp.stack(values))
+
+
 def solution(mesh):
     in_specs = (
         P("rep", "fsdp", "patch"),
@@ -155,4 +434,6 @@
         P("rep", "fsdp", "patch"),
     )
     out_specs = (P("rep", "fsdp", "patch"), P("rep", "fsdp", "patch"), P("rep", "fsdp", "patch"))
-    return jax.shard_map(shards, mesh=mesh, in_specs=in_specs, out_specs=out_specs, check_vma=False)
+    four = (mesh.shape["rep"], mesh.shape["fsdp"], mesh.shape["patch"]) == (2, 4, 4)
+    step = shards_four if four else shards_any
+    return jax.shard_map(step, mesh=mesh, in_specs=in_specs, out_specs=out_specs, check_vma=False)

time: 434 us -> 257 us (0.59)
  waiting for transfers between devices: 354 us -> 160 us
  Pallas kernels: 0 us -> 47.4 us
  starting transfers between devices: 0.23 us -> 29.4 us
  matrix products: 26.6 us -> 0.24 us
  blocking collectives: 14.9 us -> 0 us
  between operations: 14.4 us -> 0.92 us
    all_gather x5 -> x0, waiting for transfers between devices: 295 us -> none  [the longest x1 168 us: shards(): lax.all_gather(qkv_weight, 'fsdp', axis=0, tiled=True)]
    ppermute x0 -> x31, waiting for transfers between devices: none -> 160 us  [the longest x13 82 us: to_z(): return lax.ppermute(v, 'patch', [(i, i ^ d) for i in range(4)])]
    reduce_scatter x1 -> x0, waiting for transfers between devices: 57.3 us -> none  [shards(): lax.psum_scatter(terms.astype(jnp.bfloat16), 'patch', scatter_dimension=2...]
    pallas_call x0 -> x6, Pallas kernels: none -> 47.4 us  [the longest x2 22.3 us: run_attend(): pl.pallas_call(attend_kernel, grid_spec=pltpu.PrefetchScalarGridSpec(num_...]
    ppermute x0 -> x31, starting transfers between devices: none -> 29.4 us  [the longest x13 16.7 us: to_z(): return lax.ppermute(v, 'patch', [(i, i ^ d) for i in range(4)])]
    dot_general x7 -> x1, matrix products: 26.6 us -> 0.24 us  [pick_rows(): jnp.einsum('st,tcf->scf', onehot, modulation, preferred_element_type=jnp....]
    all_gather x1 -> x0, blocking collectives: 14.9 us -> none  [shards(): lax.all_gather(picked, 'patch', axis=2, tiled=True)]
    another operation x1 -> x10, other arithmetic: 0.68 us -> 7.25 us  [the longest x4 2.88 us: shards_four(): return (jnp.stack(outs), jnp.stack(keys), jnp.stack(values))]
  transfers between devices with their start and end apart: 6 -> 31, of which waited for: 5 -> 18; matrix products, arithmetic and copies ran while one was open for 9% -> 4% of each run, Pallas kernels for 0% -> 15%
where the time goes in v1:
time: 257 us
  waiting for transfers between devices  160 us (62%)
  Pallas kernels  47.4 us (18%)
  starting transfers between devices  29.4 us (11%)
  other arithmetic  11 us (4%)
  local copies, waits for them, and re-layouts  7.48 us (3%)
    ppermute x13, waiting for transfers between devices, to_z(): return lax.ppermute(v, 'patch', [(i, i ^ d) for i in range(4)])  82 us
    ppermute x17, waiting for transfers between devices, to_f(): return lax.ppermute(v, 'fsdp', [(i, i ^ d) for i in range(4)])  77.6 us
    pallas_call x2, Pallas kernels, run_attend(): pl.pallas_call(attend_kernel, grid_spec=pltpu.PrefetchScalarGridSpec(num_...  22.3 us
    ppermute x13, starting transfers between devices, to_z(): return lax.ppermute(v, 'patch', [(i, i ^ d) for i in range(4)])  16.7 us
    pallas_call x2, Pallas kernels, run_project(): pl.pallas_call(project_kernel, grid=(3,), in_specs=[vmem] * 4 + [pl.Block...  16.4 us
    ppermute x17, starting transfers between devices, to_f(): return lax.ppermute(v, 'fsdp', [(i, i ^ d) for i in range(4)])  11.1 us
    pallas_call x2, Pallas kernels, run_norm(): pl.pallas_call(norm_kernel, in_specs=[pl.BlockSpec(memory_space=pltpu.SME...  8.65 us
  transfers between devices with their start and end apart: 31, of which 18 were waited for; matrix products, arithmetic and copies ran while one was open for 4% of the time, Pallas kernels for 15%

profile of v1, /device:TPU:0, one launch (start us, length us, event | category | flops | bytes accessed | tf_op | source)
XLA Modules:
  0.0 256.7 jit_solution(4320872589827891035)
XLA Ops:
  2.9 2.9 %collective-permute-start.2 = (bf16[2,2,128,768]{3,2,1,0:T(8,128)(2,1)}, bf16[2,2,128,768]{3,2,1,0:T(8,128)(2,1)}, u32[]{:S(2)}, u32[]{:S(2)}) collective-permute-start(bf16[2,2,128,768]{3,2,1,0:T(8,128)(2,1)} %pad_maximum_fusion), channel_id=1, source_target_pairs={{0,8},{4,12},{8,0},{12,4},{1,9},{5,13},{9,1},{13,5},{2,10},{6,14},... | collective-permute-start | bytes 2359304 | tf_op jit(solution)/shard_map/ppermute | solution.py:346
  6.6 2.6 %collective-permute-start.1 = (bf16[128,1536]{1,0:T(8,128)(2,1)}, bf16[128,1536]{1,0:T(8,128)(2,1)}, u32[]{:S(2)}, u32[]{:S(2)}) collective-permute-start(bf16[128,1536]{1,0:T(8,128)(2,1)} %get-tuple-element.65.own), channel_id=1, source_target_pairs={{0,2},{1,3},{2,0},{3,1},{4,6},{5,7},{6,4},{7,5},{8,10},{9,11},{10,... | collective-permute-start | bytes 1179656 | tf_op jit(solution)/shard_map/ppermute | solution.py:352
  10.6 13.0 %collective-permute-done.2.s_x = bf16[2,2,128,768]{3,2,1,0:T(8,128)(2,1)} collective-permute-done((bf16[2,2,128,768]{3,2,1,0:T(8,128)(2,1)}, bf16[2,2,128,768]{3,2,1,0:T(8,128)(2,1)}, u32[]{:S(2)}, u32[]{:S(2)}) %collective-permute-start.2) | collective-permute-done | bytes 786464 | tf_op jit(solution)/shard_map/ppermute | solution.py:346
  25.5 2.7 %collective-permute-start.5 = (bf16[2,2,1536]{2,1,0:T(2,128)(2,1)S(1)}, bf16[2,2,1536]{2,1,0:T(2,128)(2,1)S(1)}, u32[]{:S(2)}, u32[]{:S(2)}) collective-permute-start(bf16[2,2,1536]{2,1,0:T(2,128)(2,1)S(1)} %get-tuple-element.70), channel_id=1, source_target_pairs={{0,2},{1,3},{2,0},{3,1},{4,6},{5,7},{6,4},{7,5},{8,10},{9,11},{10,... | collective-permute-start | bytes 36872 | tf_op jit(solution)/shard_map/ppermute | solution.py:352
  34.6 8.1 %collective-permute-done.one = bf16[128,1536]{1,0:T(8,128)(2,1)S(1)} collective-permute-done((bf16[128,1536]{1,0:T(8,128)(2,1)}, bf16[128,1536]{1,0:T(8,128)(2,1)S(1)}, u32[]{:S(2)}, u32[]{:S(2)}) %collective-permute-start) | collective-permute-done | bytes 393248 | tf_op jit(solution)/shard_map/ppermute | solution.py:352
  42.6 5.8 %collective-permute-done.3.three = bf16[128,1536]{1,0:T(8,128)(2,1)S(1)} collective-permute-done((bf16[128,1536]{1,0:T(8,128)(2,1)}, bf16[128,1536]{1,0:T(8,128)(2,1)S(1)}, u32[]{:S(2)}, u32[]{:S(2)}) %collective-permute-start.3) | collective-permute-done | bytes 393248 | tf_op jit(solution)/shard_map/ppermute | solution.py:352
  49.1 4.3 %norm.2 = (bf16[128,1536]{1,0:T(8,128)(2,1)}, bf16[128,1536]{1,0:T(8,128)(2,1)}, bf16[128,1536]{1,0:T(8,128)(2,1)}, bf16[128,1536]{1,0:T(8,128)(2,1)}) custom-call(s32[2]{0:T(128)} %pad_add_fusion.key.at, bf16[128,1536]{1,0:T(8,128)(2,1)} %get-tuple-element.65.own, bf16[128,1536]{1,0:T(8,128)(2,1)} %copy-done.13, ...), custom_call_target="tpu_custom_call" | custom-call | flops 11796480 | bytes 3145728 | tf_op jit(solution)/shard_map/norm/pallas_call | solution.py:259
  55.4 10.3 %collective-permute-done.9.over = bf16[128,1536]{1,0:T(8,128)(2,1)S(1)} collective-permute-done((bf16[128,1536]{1,0:T(8,128)(2,1)}, bf16[128,1536]{1,0:T(8,128)(2,1)S(1)}, u32[]{:S(2)}, u32[]{:S(2)}) %collective-permute-start.9) | collective-permute-done | bytes 393248 | tf_op jit(solution)/shard_map/ppermute | solution.py:346
  65.7 7.5 %collective-permute-done.10.cross = bf16[128,1536]{1,0:T(8,128)(2,1)S(1)} collective-permute-done((bf16[128,1536]{1,0:T(8,128)(2,1)}, bf16[128,1536]{1,0:T(8,128)(2,1)S(1)}, u32[]{:S(2)}, u32[]{:S(2)}) %collective-permute-start.10) | collective-permute-done | bytes 393248 | tf_op jit(solution)/shard_map/ppermute | solution.py:346
  73.9 8.2 %project.2 = (f32[2,128,2304]{2,1,0:T(8,128)}, f32[2,128,2304]{2,1,0:T(8,128)}) custom-call(bf16[128,1536]{1,0:T(8,128)(2,1)} %get-tuple-element.33.own, bf16[128,1536]{1,0:T(8,128)(2,1)} %copy-done.28, bf16[128,1536]{1,0:T(8,128)(2,1)} %copy-done.29, bf16[128,1536]{1,0:T(8,128)(2,1)} %copy-done.30, bf16[3,1536,768]{2,1,0:T(8,128)(2,1)} %bitcast.89), custom_call_target="tpu_custom_call" | custom-call | flops 3623878656 | bytes 11796480 | tf_op jit(solution)/shard_map/project/pallas_call | solution.py:279
  82.3 2.5 collective-permute-start.22
  85.7 17.3 %collective-permute-done.22.two = bf16[128,1536]{1,0:T(8,128)(2,1)S(1)} collective-permute-done((bf16[128,1536]{1,0:T(8,128)(2,1)S(1)}, bf16[128,1536]{1,0:T(8,128)(2,1)S(1)}, u32[]{:S(2)}, u32[]{:S(2)}) %collective-permute-start.22) | collective-permute-done | bytes 393248 | tf_op jit(solution)/shard_map/ppermute | solution.py:352
  103.2 10.2 %collective-permute-done.23.three = bf16[128,1536]{1,0:T(8,128)(2,1)S(1)} collective-permute-done((bf16[128,1536]{1,0:T(8,128)(2,1)S(1)}, bf16[128,1536]{1,0:T(8,128)(2,1)S(1)}, u32[]{:S(2)}, u32[]{:S(2)}) %collective-permute-start.23) | collective-permute-done | bytes 393248 | tf_op jit(solution)/shard_map/ppermute | solution.py:352
  114.1 4.3 %norm.3 = (bf16[128,1536]{1,0:T(8,128)(2,1)}, bf16[128,1536]{1,0:T(8,128)(2,1)}, bf16[128,1536]{1,0:T(8,128)(2,1)}, bf16[128,1536]{1,0:T(8,128)(2,1)}) custom-call(s32[2]{0:T(128)} %pad_add_fusion.key.at, bf16[128,1536]{1,0:T(8,128)(2,1)} %copy-done.8, bf16[128,1536]{1,0:T(8,128)(2,1)} %copy-done.15, bf16[128,1536]{1,0:T(8,128)(2,1)} %copy-done.14, ...), custom_call_target="tpu_custom_call" | custom-call | flops 11796480 | bytes 3145728 | tf_op jit(solution)/shard_map/norm/pallas_call | solution.py:259
  121.9 8.7 %collective-permute-done.25.over = bf16[128,1536]{1,0:T(8,128)(2,1)S(1)} collective-permute-done((bf16[128,1536]{1,0:T(8,128)(2,1)}, bf16[128,1536]{1,0:T(8,128)(2,1)S(1)}, u32[]{:S(2)}, u32[]{:S(2)}) %collective-permute-start.25) | collective-permute-done | bytes 393248 | tf_op jit(solution)/shard_map/ppermute | solution.py:346
  130.6 7.6 %collective-permute-done.26.cross = bf16[128,1536]{1,0:T(8,128)(2,1)S(1)} collective-permute-done((bf16[128,1536]{1,0:T(8,128)(2,1)}, bf16[128,1536]{1,0:T(8,128)(2,1)S(1)}, u32[]{:S(2)}, u32[]{:S(2)}) %collective-permute-start.26) | collective-permute-done | bytes 393248 | tf_op jit(solution)/shard_map/ppermute | solution.py:346
  139.0 8.3 %project.3 = (f32[2,128,2304]{2,1,0:T(8,128)}, f32[2,128,2304]{2,1,0:T(8,128)}) custom-call(bf16[128,1536]{1,0:T(8,128)(2,1)} %get-tuple-element.47.own, bf16[128,1536]{1,0:T(8,128)(2,1)} %copy-done.25, bf16[128,1536]{1,0:T(8,128)(2,1)} %copy-done.26, bf16[128,1536]{1,0:T(8,128)(2,1)} %copy-done.27, bf16[3,1536,768]{2,1,0:T(8,128)(2,1)} %bitcast.90), custom_call_target="tpu_custom_call" | custom-call | flops 3623878656 | bytes 11796480 | tf_op jit(solution)/shard_map/project/pallas_call | solution.py:279
  150.7 3.8 %collective-permute-done.15.s_d = bf16[2,2,128,768]{3,2,1,0:T(8,128)(2,1)S(1)} collective-permute-done((bf16[2,2,128,768]{3,2,1,0:T(8,128)(2,1)}, bf16[2,2,128,768]{3,2,1,0:T(8,128)(2,1)S(1)}, u32[]{:S(2)}, u32[]{:S(2)}) %collective-permute-start.15) | collective-permute-done | bytes 786464 | tf_op jit(solution)/shard_map/ppermute | solution.py:346
  157.0 12.8 %collective-permute-done.13.over = bf16[128,2304]{1,0:T(8,128)(2,1)S(1)} collective-permute-done((bf16[128,2304]{1,0:T(8,128)(2,1)S(1)}, bf16[128,2304]{1,0:T(8,128)(2,1)S(1)}, u32[]{:S(2)}, u32[]{:S(2)}) %collective-permute-start.13) | collective-permute-done | bytes 589856 | tf_op jit(solution)/shard_map/ppermute | solution.py:346
  170.7 11.1 %attend.2 = (bf16[128,768]{1,0:T(8,128)(2,1)}, bf16[128,768]{1,0:T(8,128)(2,1)}, bf16[2,128,1536]{2,1,0:T(8,128)(2,1)}, bf16[2,128,1536]{2,1,0:T(8,128)(2,1)}) custom-call(s32[2]{0:T(128)} %pad_add_fusion.key.at, f32[2,128,2304]{2,1,0:T(8,128)} %get-tuple-element.40.kept, f32[2,128,2304]{2,1,0:T(8,128)} %collective-permute-done.11.back, ...), custom_call_target="tpu_custom_call" | custom-call | flops 1409286144 | bytes 14155776 | tf_op jit(solution)/shard_map/attend/pallas_call | solution.py:304
  184.1 13.7 %collective-permute-done.28.over = bf16[128,2304]{1,0:T(8,128)(2,1)S(1)} collective-permute-done((bf16[128,2304]{1,0:T(8,128)(2,1)S(1)}, bf16[128,2304]{1,0:T(8,128)(2,1)S(1)}, u32[]{:S(2)}, u32[]{:S(2)}) %collective-permute-start.28) | collective-permute-done | bytes 589856 | tf_op jit(solution)/shard_map/ppermute | solution.py:346
  198.7 11.2 %attend.3 = (bf16[128,768]{1,0:T(8,128)(2,1)}, bf16[128,768]{1,0:T(8,128)(2,1)}, bf16[2,128,1536]{2,1,0:T(8,128)(2,1)}, bf16[2,128,1536]{2,1,0:T(8,128)(2,1)}) custom-call(s32[2]{0:T(128)} %pad_add_fusion.key.at, f32[2,128,2304]{2,1,0:T(8,128)} %get-tuple-element.53.kept, f32[2,128,2304]{2,1,0:T(8,128)} %collective-permute-done.27.back, ...), custom_call_target="tpu_custom_call" | custom-call | flops 1409286144 | bytes 14155776 | tf_op jit(solution)/shard_map/attend/pallas_call | solution.py:304
  213.5 22.5 %collective-permute-done.29 = bf16[2,128,1536]{2,1,0:T(8,128)(2,1)S(1)} collective-permute-done((bf16[2,128,1536]{2,1,0:T(8,128)(2,1)}, bf16[2,128,1536]{2,1,0:T(8,128)(2,1)S(1)}, u32[]{:S(2)}, u32[]{:S(2)}) %collective-permute-start.29) | collective-permute-done | bytes 786464 | tf_op jit(solution)/shard_map/ppermute | solution.py:352
  239.0 16.3 %collective-permute-done.30 = bf16[128,1536]{1,0:T(8,128)(2,1)S(1)} collective-permute-done((bf16[128,1536]{1,0:T(8,128)(2,1)S(1)}, bf16[128,1536]{1,0:T(8,128)(2,1)S(1)}, u32[]{:S(2)}, u32[]{:S(2)}) %collective-permute-start.30) | collective-permute-done | bytes 393248 | tf_op jit(solution)/shard_map/ppermute | solution.py:352
  (135 shorter events, 40.0 us)
Async XLA Ops:
  2.9 20.8 %collective-permute-start.2 = (bf16[2,2,128,768]{3,2,1,0:T(8,128)(2,1)}, bf16[2,2,128,768]{3,2,1,0:T(8,128)(2,1)}, u32[]{:S(2)}, u32[]{:S(2)}) collective-permute-start(bf16[2,2,128,768]{3,2,1,0:T(8,128)(2,1)} %pad_maximum_fusion), channel_id=1, source_target_pairs={{0,8},{4,12},{8,0},{12,4},{1,9},{5,13},{9,1},{13,5},{2,10},{6,14},... | collective-permute-start | bytes 2359304 | tf_op jit(solution)/shard_map/ppermute | solution.py:346
  6.6 27.2 %collective-permute-start.1 = (bf16[128,1536]{1,0:T(8,128)(2,1)}, bf16[128,1536]{1,0:T(8,128)(2,1)}, u32[]{:S(2)}, u32[]{:S(2)}) collective-permute-start(bf16[128,1536]{1,0:T(8,128)(2,1)} %get-tuple-element.65.own), channel_id=1, source_target_pairs={{0,2},{1,3},{2,0},{3,1},{4,6},{5,7},{6,4},{7,5},{8,10},{9,11},{10,... | collective-permute-start | bytes 1179656 | tf_op jit(solution)/shard_map/ppermute | solution.py:352
  23.7 29.8 %collective-permute-start.8 = (bf16[384,1536]{1,0:T(8,128)(2,1)}, bf16[384,1536]{1,0:T(8,128)(2,1)}, u32[]{:S(2)}, u32[]{:S(2)}) collective-permute-start(bf16[384,1536]{1,0:T(8,128)(2,1)} %constant_dynamic-slice_fusion), channel_id=1, source_target_pairs={{0,8},{4,12},{8,0},{12,4},{1,9},{5,13},{9,1},{13,5},{2,10},{6,14},... | collective-permute-start | bytes 3538952 | tf_op jit(solution)/shard_map/ppermute | solution.py:346
  30.4 12.3 %collective-permute-start = (bf16[128,1536]{1,0:T(8,128)(2,1)}, bf16[128,1536]{1,0:T(8,128)(2,1)S(1)}, u32[]{:S(2)}, u32[]{:S(2)}) collective-permute-start(bf16[128,1536]{1,0:T(8,128)(2,1)} %get-tuple-element.65.own), channel_id=1, source_target_pairs={{0,1},{1,0},{2,3},{3,2},{4,5},{5,4},{6,7},{7,6},{8,9},{9,8},{10,11... | collective-permute-start | bytes 1179656 | tf_op jit(solution)/shard_map/ppermute | solution.py:352
  33.8 14.6 %collective-permute-start.3 = (bf16[128,1536]{1,0:T(8,128)(2,1)}, bf16[128,1536]{1,0:T(8,128)(2,1)S(1)}, u32[]{:S(2)}, u32[]{:S(2)}) collective-permute-start(bf16[128,1536]{1,0:T(8,128)(2,1)} %collective-permute-done.1.two), channel_id=1, source_target_pairs={{0,1},{1,0},{2,3},{3,2},{4,5},{5,4},{6,7},{7,6},{8,9},{9,8},{10,11... | collective-permute-start | bytes 1179656 | tf_op jit(solution)/shard_map/ppermute | solution.py:352
  53.5 12.2 %collective-permute-start.9 = (bf16[128,1536]{1,0:T(8,128)(2,1)}, bf16[128,1536]{1,0:T(8,128)(2,1)S(1)}, u32[]{:S(2)}, u32[]{:S(2)}) collective-permute-start(bf16[128,1536]{1,0:T(8,128)(2,1)} %get-tuple-element.37), channel_id=1, source_target_pairs={{0,8},{4,12},{8,0},{12,4},{1,9},{5,13},{9,1},{13,5},{2,10},{6,14},... | collective-permute-start | bytes 1179656 | tf_op jit(solution)/shard_map/ppermute | solution.py:346
  54.1 19.1 %collective-permute-start.10 = (bf16[128,1536]{1,0:T(8,128)(2,1)}, bf16[128,1536]{1,0:T(8,128)(2,1)S(1)}, u32[]{:S(2)}, u32[]{:S(2)}) collective-permute-start(bf16[128,1536]{1,0:T(8,128)(2,1)} %get-tuple-element.39), channel_id=1, source_target_pairs={{0,12},{4,8},{8,4},{12,0},{1,13},{5,9},{9,5},{13,1},{2,14},{6,10},... | collective-permute-start | bytes 1179656 | tf_op jit(solution)/shard_map/ppermute | solution.py:346
  82.1 66.8 %collective-permute-start.11 = (f32[2,128,2304]{2,1,0:T(8,128)}, f32[2,128,2304]{2,1,0:T(8,128)}, u32[]{:S(2)}, u32[]{:S(2)}) collective-permute-start(f32[2,128,2304]{2,1,0:T(8,128)} %get-tuple-element.41), channel_id=1, source_target_pairs={{0,4},{4,0},{8,12},{12,8},{1,5},{5,1},{9,13},{13,9},{2,6},{6,2},{1... | collective-permute-start | bytes 7077896 | tf_op jit(solution)/shard_map/ppermute | solution.py:346
  82.3 20.7 %collective-permute-start.22 = (bf16[128,1536]{1,0:T(8,128)(2,1)S(1)}, bf16[128,1536]{1,0:T(8,128)(2,1)S(1)}, u32[]{:S(2)}, u32[]{:S(2)}) collective-permute-start(bf16[128,1536]{1,0:T(8,128)(2,1)S(1)} %get-tuple-element.45.own), channel_id=1, source_target_pairs={{0,2},{1,3},{2,0},{3,1},{4,6},{5,7},{6,4},{7,5},{8,10},{9,11},{10,... | collective-permute-start | bytes 1179656 | tf_op jit(solution)/shard_map/ppermute | solution.py:352
  84.9 18.3 %collective-permute-start.21 = (bf16[128,1536]{1,0:T(8,128)(2,1)S(1)}, bf16[128,1536]{1,0:T(8,128)(2,1)S(1)}, u32[]{:S(2)}, u32[]{:S(2)}) collective-permute-start(bf16[128,1536]{1,0:T(8,128)(2,1)S(1)} %get-tuple-element.45.own), channel_id=1, source_target_pairs={{0,1},{1,0},{2,3},{3,2},{4,5},{5,4},{6,7},{7,6},{8,9},{9,8},{10,11... | collective-permute-start | bytes 1179656 | tf_op jit(solution)/shard_map/ppermute | solution.py:352
  103.0 10.4 %collective-permute-start.23 = (bf16[128,1536]{1,0:T(8,128)(2,1)S(1)}, bf16[128,1536]{1,0:T(8,128)(2,1)S(1)}, u32[]{:S(2)}, u32[]{:S(2)}) collective-permute-start(bf16[128,1536]{1,0:T(8,128)(2,1)S(1)} %collective-permute-done.22.two), channel_id=1, source_target_pairs={{0,1},{1,0},{2,3},{3,2},{4,5},{5,4},{6,7},{7,6},{8,9},{9,8},{10,11... | collective-permute-start | bytes 1179656 | tf_op jit(solution)/shard_map/ppermute | solution.py:352
  118.5 12.1 %collective-permute-start.25 = (bf16[128,1536]{1,0:T(8,128)(2,1)}, bf16[128,1536]{1,0:T(8,128)(2,1)S(1)}, u32[]{:S(2)}, u32[]{:S(2)}) collective-permute-start(bf16[128,1536]{1,0:T(8,128)(2,1)} %get-tuple-element.50), channel_id=1, source_target_pairs={{0,8},{4,12},{8,0},{12,4},{1,9},{5,13},{9,1},{13,5},{2,10},{6,14},... | collective-permute-start | bytes 1179656 | tf_op jit(solution)/shard_map/ppermute | solution.py:346
  119.0 19.2 %collective-permute-start.26 = (bf16[128,1536]{1,0:T(8,128)(2,1)}, bf16[128,1536]{1,0:T(8,128)(2,1)S(1)}, u32[]{:S(2)}, u32[]{:S(2)}) collective-permute-start(bf16[128,1536]{1,0:T(8,128)(2,1)} %get-tuple-element.52), channel_id=1, source_target_pairs={{0,12},{4,8},{8,4},{12,0},{1,13},{5,9},{9,5},{13,1},{2,14},{6,10},... | collective-permute-start | bytes 1179656 | tf_op jit(solution)/shard_map/ppermute | solution.py:346
  120.3 28.5 %collective-permute-start.12 = (bf16[384,1536]{1,0:T(8,128)(2,1)}, bf16[384,1536]{1,0:T(8,128)(2,1)}, u32[]{:S(2)}, u32[]{:S(2)}) collective-permute-start(bf16[384,1536]{1,0:T(8,128)(2,1)} %collective-permute-done.8.o_x), channel_id=1, source_target_pairs={{0,16},{16,0},{1,17},{17,1},{2,18},{18,2},{3,19},{19,3},{4,20},{20... | collective-permute-start | bytes 3538952 | tf_op jit(solution)/shard_map/ppermute | solution.py:349
  121.9 26.1 %collective-permute-start.14 = (bf16[2,2,128,768]{3,2,1,0:T(8,128)(2,1)}, bf16[2,2,128,768]{3,2,1,0:T(8,128)(2,1)}, u32[]{:S(2)}, u32[]{:S(2)}) collective-permute-start(bf16[2,2,128,768]{3,2,1,0:T(8,128)(2,1)} %pad_maximum_fusion), channel_id=1, source_target_pairs={{0,4},{4,0},{8,12},{12,8},{1,5},{5,1},{9,13},{13,9},{2,6},{6,2},{1... | collective-permute-start | bytes 2359304 | tf_op jit(solution)/shard_map/ppermute | solution.py:346
  130.6 26.4 %collective-permute-start.16 = (bf16[768,1536]{1,0:T(8,128)(2,1)S(1)}, bf16[768,1536]{1,0:T(8,128)(2,1)S(1)}, u32[]{:S(2)}, u32[]{:S(2)}) collective-permute-start(bf16[768,1536]{1,0:T(8,128)(2,1)S(1)} %copy-done.1), channel_id=1, source_target_pairs={{0,4},{4,0},{8,12},{12,8},{1,5},{5,1},{9,13},{13,9},{2,6},{6,2},{1... | collective-permute-start | bytes 7077896 | tf_op jit(solution)/shard_map/ppermute | solution.py:346
  147.3 34.8 %collective-permute-start.27 = (f32[2,128,2304]{2,1,0:T(8,128)}, f32[2,128,2304]{2,1,0:T(8,128)}, u32[]{:S(2)}, u32[]{:S(2)}) collective-permute-start(f32[2,128,2304]{2,1,0:T(8,128)} %get-tuple-element.54), channel_id=1, source_target_pairs={{0,4},{4,0},{8,12},{12,8},{1,5},{5,1},{9,13},{13,9},{2,6},{6,2},{1... | collective-permute-start | bytes 7077896 | tf_op jit(solution)/shard_map/ppermute | solution.py:346
  148.8 8.2 %collective-permute-start.18 = (bf16[384,1536]{1,0:T(8,128)(2,1)}, bf16[384,1536]{1,0:T(8,128)(2,1)}, u32[]{:S(2)}, u32[]{:S(2)}) collective-permute-start(bf16[384,1536]{1,0:T(8,128)(2,1)} %collective-permute-done.12.o_xo), channel_id=1, source_target_pairs={{0,4},{4,0},{8,12},{12,8},{1,5},{5,1},{9,13},{13,9},{2,6},{6,2},{1... | collective-permute-start | bytes 3538952 | tf_op jit(solution)/shard_map/ppermute | solution.py:346
  154.5 15.4 %collective-permute-start.13 = (bf16[128,2304]{1,0:T(8,128)(2,1)S(1)}, bf16[128,2304]{1,0:T(8,128)(2,1)S(1)}, u32[]{:S(2)}, u32[]{:S(2)}) collective-permute-start(bf16[128,2304]{1,0:T(8,128)(2,1)S(1)} %fusion.10), channel_id=1, source_target_pairs={{0,8},{4,12},{8,0},{12,4},{1,9},{5,13},{9,1},{13,5},{2,10},{6,14},... | collective-permute-start | bytes 1769480 | tf_op jit(solution)/shard_map/ppermute | solution.py:346
  181.8 29.7 %collective-permute-start.19 = (bf16[2,128,1536]{2,1,0:T(8,128)(2,1)}, bf16[2,128,1536]{2,1,0:T(8,128)(2,1)S(1)}, u32[]{:S(2)}, u32[]{:S(2)}) collective-permute-start(bf16[2,128,1536]{2,1,0:T(8,128)(2,1)} %get-tuple-element.44), channel_id=1, source_target_pairs={{0,1},{1,0},{2,3},{3,2},{4,5},{5,4},{6,7},{7,6},{8,9},{9,8},{10,11... | collective-permute-start | bytes 2359304 | tf_op jit(solution)/shard_map/ppermute | solution.py:352
  183.5 14.3 %collective-permute-start.28 = (bf16[128,2304]{1,0:T(8,128)(2,1)S(1)}, bf16[128,2304]{1,0:T(8,128)(2,1)S(1)}, u32[]{:S(2)}, u32[]{:S(2)}) collective-permute-start(bf16[128,2304]{1,0:T(8,128)(2,1)S(1)} %fusion.11), channel_id=1, source_target_pairs={{0,8},{4,12},{8,0},{12,4},{1,9},{5,13},{9,1},{13,5},{2,10},{6,14},... | collective-permute-start | bytes 1769480 | tf_op jit(solution)/shard_map/ppermute | solution.py:346
  209.8 26.2 %collective-permute-start.29 = (bf16[2,128,1536]{2,1,0:T(8,128)(2,1)}, bf16[2,128,1536]{2,1,0:T(8,128)(2,1)S(1)}, u32[]{:S(2)}, u32[]{:S(2)}) collective-permute-start(bf16[2,128,1536]{2,1,0:T(8,128)(2,1)} %get-tuple-element.56), channel_id=1, source_target_pairs={{0,1},{1,0},{2,3},{3,2},{4,5},{5,4},{6,7},{7,6},{8,9},{9,8},{10,11... | collective-permute-start | bytes 2359304 | tf_op jit(solution)/shard_map/ppermute | solution.py:352
  211.8 27.2 %collective-permute-start.20 = (bf16[128,1536]{1,0:T(8,128)(2,1)S(1)}, bf16[128,1536]{1,0:T(8,128)(2,1)S(1)}, u32[]{:S(2)}, u32[]{:S(2)}) collective-permute-start(bf16[128,1536]{1,0:T(8,128)(2,1)S(1)} %fusion.13), channel_id=1, source_target_pairs={{0,2},{1,3},{2,0},{3,1},{4,6},{5,7},{6,4},{7,5},{8,10},{9,11},{10,... | collective-permute-start | bytes 1179656 | tf_op jit(solution)/shard_map/ppermute | solution.py:352
  236.3 19.0 %collective-permute-start.30 = (bf16[128,1536]{1,0:T(8,128)(2,1)S(1)}, bf16[128,1536]{1,0:T(8,128)(2,1)S(1)}, u32[]{:S(2)}, u32[]{:S(2)}) collective-permute-start(bf16[128,1536]{1,0:T(8,128)(2,1)S(1)} %fusion.15), channel_id=1, source_target_pairs={{0,2},{1,3},{2,0},{3,1},{4,6},{5,7},{6,4},{7,5},{8,10},{9,11},{10,... | collective-permute-start | bytes 1179656 | tf_op jit(solution)/shard_map/ppermute | solution.py:352
  (39 other events, 378.9 us)

commit v2 on v1

--- a/solution.py
+++ b/solution.py
@@ -149,41 +149,60 @@
     return (block_out, fresh_keys.reshape(samples, rows, local_width), fresh_flat)
 
 
-def norm_kernel(key, own, one, two, three, turns, *rest):
-    outs, held = rest[:4], rest[4]
-    blocks = (own, one, two, three)
-    width = 4 * own.shape[1]
-    mean = sum(jnp.sum(b[...].astype(jnp.float32), axis=-1, keepdims=True) for b in blocks) / width
-    spread = (
-        sum(
-            jnp.sum(jnp.square(b[...].astype(jnp.float32) - mean), axis=-1, keepdims=True)
-            for b in blocks
-        )
-        / width
-    )
+def pack_kernel(timestep, latent, modulation, packed, gates):
+    samples, feats = gates.shape
+    rows = latent.shape[1]
+    packed[:rows] = latent[0]
+    level = lax.broadcasted_iota(jnp.int32, modulation.shape[1:], 0)
+    picked = []
+    for s in range(samples):
+        here = level == timestep[s]
+        for k in range(3):
+            kept = jnp.where(here, modulation[k].astype(jnp.float32), 0.0)
+            picked.append(jnp.sum(kept, axis=0, keepdims=True))
+        gates[s : s + 1] = picked.pop()
+    fill = jnp.zeros((packed.shape[0] - rows - 2 * samples, feats), jnp.float32)
+    packed[rows:] = jnp.concatenate([*picked, fill], axis=0).astype(jnp.bfloat16)
+
+
+def norm_kernel(s, key, *refs):
+    blocks, turns, outs, held = refs[:4], refs[4:8], refs[8:12], refs[12]
+    rows, feats = outs[0].shape
+    mean = sum(
+        jnp.sum(b[:rows].astype(jnp.float32), axis=-1, keepdims=True) for b in blocks
+    ) / (4 * feats)
+    spread = sum(
+        jnp.sum(jnp.square(b[:rows].astype(jnp.float32) - mean), axis=-1, keepdims=True)
+        for b in blocks
+    ) / (4 * feats)
     rate = lax.rsqrt(spread + EPS)
-    for r, block in enumerate(blocks):
-        shift = turns[r, 0:1].astype(jnp.float32)
-        scale = turns[r, 1:2].astype(jnp.float32)
-        centered = block[...].astype(jnp.float32) - mean
+    for r, (block, turn) in enumerate(zip(blocks, turns)):
+        low = turn[rows:].astype(jnp.float32)
+        shift = low[2 * s : 2 * s + 1]
+        scale = low[2 * s + 1 : 2 * s + 2]
+        centered = block[:rows].astype(jnp.float32) - mean
         held[r ^ key[0]] = (centered * rate * (1.0 + scale) + shift).astype(jnp.bfloat16)
     for j in range(4):
         outs[j][...] = held[j]
 
 
-def project_kernel(own, pair, over, cross, weight, kept, sent):
-    rows = own.shape[0]
-    every = jnp.concatenate([own[...], over[...], pair[...], cross[...]], axis=0)
-    product = jnp.dot(every, weight[0], preferred_element_type=jnp.float32)
-    for i in range(2):
-        kept[i] = product[i * rows : (i + 1) * rows]
-        sent[i] = product[(i + 2) * rows : (i + 3) * rows]
+def project_kernel(first, second, weight, out, held):
+    rows = first.shape[0]
+
+    @pl.when(pl.program_id(0) == 0)
+    def _():
+        held[:rows] = first[...]
+        held[rows:] = second[...]
+
+    product = jnp.dot(held[...], weight[0], preferred_element_type=jnp.float32)
+    out[0] = product[:rows]
+    out[1] = product[rows:]
 
 
 def attend_kernel(
-    at, kept, back, over, s_pair, s_x, s_d, tables, gains,
-    o_own, o_pair, o_x, o_xo, o_d, o_do,
-    keys_out, values_out, near, far, mixed, held,
+    at, kept, back, over, k_pair, v_pair, k_x, v_x, k_d, v_d, tables, gains,
+    o_own, o_pair, o_x, o_xa, o_xb, o_d, o_da, o_db,
+    keys_out, values_out, near, far_one, far_three, mixed, held, columns, sems,
 ):
     rows, width = keys_out.shape
     size = gains.shape[1]
@@ -191,6 +210,16 @@
     factor = 1.0 / size**0.5
     lane = lax.broadcasted_iota(jnp.int32, (rows, size), 1)
     low = (lane // (size // 4)) % 2 == 0
+    rep = at[1]
+    copies = []
+    for j, refs in enumerate(((o_own,), (o_pair,), (o_x, o_xa, o_xb), (o_d, o_da, o_db))):
+        start = 0
+        for ref in refs:
+            part = columns.at[j, start : start + ref.shape[0]]
+            copy = pltpu.make_async_copy(ref, part, sems.at[len(copies)])
+            copy.start()
+            copies.append(copy)
+            start += ref.shape[0]
 
     def summed(first):
         cols = slice(first, first + size)
@@ -210,8 +239,8 @@
         value = summed(2 * width + h * size).astype(jnp.bfloat16)
         keys_out[:, cols] = key
         values_out[:, cols] = value
-        keys = jnp.concatenate([key] + [s[0, 0, :, cols] for s in (s_pair, s_x, s_d)], axis=0)
-        seen = jnp.concatenate([value] + [s[1, 0, :, cols] for s in (s_pair, s_x, s_d)], axis=0)
+        keys = jnp.concatenate([key] + [s[0, :, cols] for s in (k_pair, k_x, k_d)], axis=0)
+        seen = jnp.concatenate([value] + [s[0, :, cols] for s in (v_pair, v_x, v_d)], axis=0)
         scores = (
             lax.dot_general(
                 query, keys, (((1,), (1,)), ((), ())), preferred_element_type=jnp.float32
@@ -225,71 +254,78 @@
         start = h * size - place * half
         mixed[place, :, start : start + size] = (product / total).astype(jnp.bfloat16)
 
-    rep = at[1]
-    for j, (first, second, one, two) in enumerate(
-        (
-            (o_own, o_own, 0, 1),
-            (o_pair, o_pair, 0, 1),
-            (o_x, o_xo, rep, 1 - rep),
-            (o_d, o_do, rep, 1 - rep),
-        )
-    ):
-        top = first[:half] if first.shape[0] == 2 * half else first[...]
-        low_rows = second[half:] if second.shape[0] == 2 * half else second[...]
-        term = jnp.dot(mixed[one], top, preferred_element_type=jnp.float32) + jnp.dot(
-            mixed[two], low_rows, preferred_element_type=jnp.float32
+    for copy in copies:
+        copy.wait()
+    for j in range(4):
+        one, two = (0, 1) if j < 2 else (rep, 1 - rep)
+        term = jnp.dot(mixed[one], columns[j, :half], preferred_element_type=jnp.float32) + jnp.dot(
+            mixed[two], columns[j, half:], preferred_element_type=jnp.float32
         )
         held[j ^ at[0]] = term.astype(jnp.bfloat16)
-    for i in range(2):
-        near[i] = held[2 * i]
-        far[i] = held[2 * i + 1]
-
-
-LIMIT = 56 * 1024 * 1024
-
-
-def params():
-    return pltpu.CompilerParams(vmem_limit_bytes=LIMIT)
-
-
-def run_norm(key, blocks, turns):
-    rows, cols = blocks[0].shape
+    near[0] = held[0]
+    near[1] = held[2]
+    far_one[...] = held[1]
+    far_three[...] = held[3]
+
+
+def params(mebibytes):
+    return pltpu.CompilerParams(vmem_limit_bytes=mebibytes * 1024 * 1024)
+
+
+def run_pack(timestep, latent, modulation):
+    samples, rows, feats = latent.shape
+    vmem = pl.BlockSpec(memory_space=pltpu.VMEM)
+    return pl.pallas_call(
+        pack_kernel,
+        in_specs=[pl.BlockSpec(memory_space=pltpu.SMEM), vmem, vmem],
+        out_specs=[vmem, vmem],
+        out_shape=[
+            jax.ShapeDtypeStruct((rows + 16, feats), jnp.bfloat16),
+            jax.ShapeDtypeStruct((samples, feats), jnp.float32),
+        ],
+        compiler_params=params(16),
+        name="pack",
+    )(timestep, latent, modulation.transpose(1, 0, 2))
+
+
+def run_norm(s, key, blocks, turns):
+    rows = blocks[-1].shape[0] if s else blocks[-1].shape[0] - 16
+    cols = blocks[0].shape[1]
     vmem = pl.BlockSpec(memory_space=pltpu.VMEM)
     shape = jax.ShapeDtypeStruct((rows, cols), jnp.bfloat16)
     return pl.pallas_call(
-        norm_kernel,
-        in_specs=[pl.BlockSpec(memory_space=pltpu.SMEM)] + [vmem] * 5,
+        functools.partial(norm_kernel, s),
+        in_specs=[pl.BlockSpec(memory_space=pltpu.SMEM)] + [vmem] * 8,
         out_specs=[vmem] * 4,
         out_shape=[shape] * 4,
         scratch_shapes=[pltpu.VMEM((4, rows, cols), jnp.bfloat16)],
-        compiler_params=params(),
+        compiler_params=params(16),
         cost_estimate=pl.CostEstimate(
             flops=60 * rows * cols, bytes_accessed=16 * rows * cols, transcendentals=0
         ),
         name="norm",
-    )(key, *blocks, turns)
-
-
-def run_project(own, pair, over, cross, weight):
-    rows, depth = own.shape
+    )(key, *blocks, *turns)
+
+
+def run_project(first, second, weight):
+    rows, depth = first.shape
     wide = weight.shape[2]
     vmem = pl.BlockSpec((rows, depth), lambda i: (0, 0))
-    out = pl.BlockSpec((2, rows, wide), lambda i: (0, 0, i))
-    shape = jax.ShapeDtypeStruct((2, rows, 3 * wide), jnp.float32)
     return pl.pallas_call(
         project_kernel,
         grid=(3,),
-        in_specs=[vmem] * 4 + [pl.BlockSpec((1, depth, wide), lambda i: (i, 0, 0))],
-        out_specs=[out, out],
-        out_shape=[shape, shape],
-        compiler_params=params(),
+        in_specs=[vmem] * 2 + [pl.BlockSpec((1, depth, wide), lambda i: (i, 0, 0))],
+        out_specs=pl.BlockSpec((2, rows, wide), lambda i: (0, 0, i)),
+        out_shape=jax.ShapeDtypeStruct((2, rows, 3 * wide), jnp.float32),
+        scratch_shapes=[pltpu.VMEM((2 * rows, depth), jnp.bfloat16)],
+        compiler_params=params(24),
         cost_estimate=pl.CostEstimate(
-            flops=24 * rows * depth * wide,
-            bytes_accessed=6 * depth * wide + 48 * rows * wide,
+            flops=12 * rows * depth * wide,
+            bytes_accessed=6 * depth * wide + 24 * rows * wide,
             transcendentals=0,
         ),
         name="project",
-    )(own, pair, over, cross, weight)
+    )(first, second, weight)
 
 
 def run_attend(s, at, kept, back, over, stale, tables, gains, columns):
@@ -298,23 +334,28 @@
     feats = columns[0].shape[1]
     full = pl.BlockSpec(memory_space=pltpu.VMEM)
     first = pl.BlockSpec((1, rows, triple), lambda i, at: (0, 0, 0))
-    seen = pl.BlockSpec((2, 1, rows, width), lambda i, at: (0, s, 0, 0))
+    seen = pl.BlockSpec((1, rows, width), lambda i, at: (s, 0, 0))
     head = jax.ShapeDtypeStruct((rows, width), jnp.bfloat16)
-    term = jax.ShapeDtypeStruct((2, rows, feats), jnp.bfloat16)
+    term = jax.ShapeDtypeStruct((rows, feats), jnp.bfloat16)
     return pl.pallas_call(
         attend_kernel,
         grid_spec=pltpu.PrefetchScalarGridSpec(
             num_scalar_prefetch=1,
             grid=(1,),
-            in_specs=[first, first, full] + [seen] * 3 + [full] * 8,
-            out_specs=[full] * 4,
+            in_specs=[first, first, full]
+            + [seen] * 6
+            + [full] * 2
+            + [pl.BlockSpec(memory_space=pl.ANY)] * 8,
+            out_specs=[full] * 5,
             scratch_shapes=[
                 pltpu.VMEM((2, rows, width // 2), jnp.bfloat16),
                 pltpu.VMEM((4, rows, feats), jnp.bfloat16),
+                pltpu.VMEM((4, width, feats), jnp.bfloat16),
+                pltpu.SemaphoreType.DMA((8,)),
             ],
         ),
-        out_shape=[head, head, term, term],
-        compiler_params=params(),
+        out_shape=[head, head, jax.ShapeDtypeStruct((2, rows, feats), jnp.bfloat16), term, term],
+        compiler_params=params(28),
         cost_estimate=pl.CostEstimate(
             flops=8 * rows * width * feats + 16 * rows * rows * width,
             bytes_accessed=8 * width * feats + 16 * rows * triple,
@@ -354,27 +395,25 @@
     def after(v, *deps):
         return lax.optimization_barrier((v, *deps))[0]
 
-    stale = jnp.stack([stale_keys, stale_values])
-    s_x = to_f(stale, 2)
-    own = [latent[s] for s in range(samples)]
-    one, two, three = [], [], []
+    packed, gate = run_pack(timestep, latent, modulation)
+    own = [packed, latent[1]]
+    two, one, three = [], [], []
     for s in range(samples):
-        start = own[s] if s == 0 else after(own[s], one[s - 1], two[s - 1])
+        start = own[s] if s == 0 else after(own[s], one[-1], two[-1])
+        two.append(to_z(start, 2))
         one.append(to_z(start, 1))
-        two.append(to_z(start, 2))
-        three.append(to_z(after(two[s], s_x), 1))
-
-    picked = pick_rows(timestep, modulation)
-    gate = picked[:, 2, :].astype(jnp.float32)[:, None, :]
-    turn = picked[:, :2]
-    turns = jnp.stack([turn] + [to_z(turn, d) for d in (1, 2, 3)])
+        three.append(to_z(two[s], 1))
+    turns = (own[0], one[0], two[0], three[0])
 
     deep = out_weight.shape[0] // 2
     o_half = lax.dynamic_slice_in_dim(out_weight, y * deep, deep, 0)
-    o_x = to_f(after(o_half, s_x), 2)
-    o_xo = to_y(o_x)
-    columns = (out_weight, to_f(out_weight, 1), o_x, o_xo, to_f(o_x, 1), to_f(o_xo, 1))
-    stale_seen = (to_f(stale, 1), s_x, to_f(s_x, 1))
+    o_x = to_f(o_half, 2)
+    k_x, v_x = to_f(after(stale_keys, o_x), 2), to_f(after(stale_values, o_x), 2)
+    o_xa = to_y(o_x[: deep // 2])
+    o_xb = to_y(after(o_x[deep // 2 :], o_xa))
+    over_x = (o_x, o_xa, o_xb)
+    columns = (out_weight, to_f(out_weight, 1), *over_x, *[to_f(v, 1) for v in over_x])
+    stale_seen = (to_f(stale_keys, 1), to_f(stale_values, 1), k_x, v_x, to_f(k_x, 1), to_f(v_x, 1))
 
     quarter = size // 4
     freq = 10000.0 ** (-jnp.arange(quarter, dtype=jnp.float32) / quarter)
@@ -393,30 +432,38 @@
     at = jnp.stack([key, y]).astype(jnp.int32)
 
     weight = qkv_weight.transpose(1, 0, 2)
-    fence = o_x
-    shared = []
+    fence = (k_x, v_x)
+    shared, normed = [], []
     for s in range(samples):
-        modded = run_norm(at, (own[s], one[s], two[s], three[s]), turns[:, s])
-        over = to_f(after(modded[2], fence), 2)
-        cross = to_f(after(modded[3], fence), 3)
-        fence = over
+        modded = run_norm(s, at, (own[s], one[s], two[s], three[s]), turns)
+        over = to_f(after(modded[2], *fence), 2)
+        cross = to_f(after(modded[3], *fence), 3)
+        fence = (over, cross)
+        normed.append(modded[0])
         shared.append((modded[0], to_f(modded[1], 1), over, cross))
+    halves, turned = [], []
+    for s in range(samples):
+        mine, pair, over, cross = shared[s]
+        cross = after(cross, over, o_xa, *normed) if s == 0 else after(cross, over, o_xb, part)
+        sent = run_project(pair, cross, weight)
+        back = to_f(sent, 1)
+        kept = run_project(mine, over, weight)
+        part = (kept[1] + back[1]).astype(jnp.bfloat16)
+        halves.append((kept, back))
+        turned.append(to_f(after(part, *turned), 2))
     keys, values, outs = [], [], []
     for s in range(samples):
-        kept, sent = run_project(*shared[s], weight)
-        back = to_f(sent, 1)
-        part = (kept[1] + back[1]).astype(jnp.bfloat16)
-        over = to_f(after(part, o_xo) if s == 0 else part, 2)
-        new_keys, new_values, near, far = run_attend(
-            s, at, kept, back, over, stale_seen, tables, gains, columns
+        kept, back = halves[s]
+        new_keys, new_values, near, far_one, far_three = run_attend(
+            s, at, kept, back, turned[s], stale_seen, tables, gains, columns
         )
         keys.append(new_keys)
         values.append(new_values)
-        come = to_z(far, 1)
-        pair = near.astype(jnp.float32) + come.astype(jnp.float32)
-        rest = to_z(pair[1].astype(jnp.bfloat16), 2)
-        attended = pair[0] + rest.astype(jnp.float32)
-        outs.append((own[s].astype(jnp.float32) + gate[s] * attended).astype(jnp.bfloat16))
+        come = to_z(far_three, 1)
+        rest = to_z((near[1].astype(jnp.float32) + come.astype(jnp.float32)).astype(jnp.bfloat16), 2)
+        come = to_z(far_one, 1)
+        attended = (near[0].astype(jnp.float32) + come.astype(jnp.float32)) + rest.astype(jnp.float32)
+        outs.append((latent[s].astype(jnp.float32) + gate[s] * attended).astype(jnp.bfloat16))
     return (jnp.stack(outs), jnp.stack(keys), jnp.stack(values))
 
 

time: 257 us -> 193 us (0.75)
  waiting for transfers between devices: 160 us -> 113 us
  Pallas kernels: 47.4 us -> 32.1 us
  other arithmetic: 11 us -> 4.22 us
  starting transfers between devices: 29.4 us -> 33.7 us
    ppermute x17 -> x21, waiting for transfers between devices: 77.6 us -> 29.3 us  [to_f(): return lax.ppermute(v, 'fsdp', [(i, i ^ d) for i in range(4)])]
    ppermute x1 -> x2, waiting for transfers between devices: 0.73 us -> 9.91 us  [to_y(): return lax.ppermute(v, 'rep', [(0, 1), (1, 0)])]
    ppermute x13 -> x12, waiting for transfers between devices: 82 us -> 74 us  [to_z(): return lax.ppermute(v, 'patch', [(i, i ^ d) for i in range(4)])]
    pallas_call x4 -> x7, Pallas kernels: 25.1 us -> 17.2 us  [the longest x4 10.1 us: run_project(): pl.pallas_call(project_kernel, grid=(3,), in_specs=[vmem] * 2 + [pl.Block...]
    pallas_call x2, Pallas kernels: 22.3 us -> 15 us  [run_attend(): pl.pallas_call(attend_kernel, grid_spec=pltpu.PrefetchScalarGridSpec(num_...]
    ppermute x17 -> x21, starting transfers between devices: 11.1 us -> 14.8 us  [to_f(): return lax.ppermute(v, 'fsdp', [(i, i ^ d) for i in range(4)])]
    ppermute x13 -> x12, starting transfers between devices: 16.7 us -> 15.8 us  [to_z(): return lax.ppermute(v, 'patch', [(i, i ^ d) for i in range(4)])]
  transfers between devices with their start and end apart: 31 -> 35, of which waited for: 18 -> 18; matrix products, arithmetic and copies ran while one was open for 4% -> 2% of each run, Pallas kernels for 15% -> 14%
where the time goes in v2:
time: 193 us; the launch traced here: 192 us
  waiting for transfers between devices  113 us (59%)
  starting transfers between devices  33.7 us (17%)
  Pallas kernels  32.1 us (17%)
  local copies, waits for them, and re-layouts  8.19 us (4%)
  other arithmetic  4.22 us (2%)
    ppermute x12, waiting for transfers between devices, to_z(): return lax.ppermute(v, 'patch', [(i, i ^ d) for i in range(4)])  74 us
    ppermute x21, waiting for transfers between devices, to_f(): return lax.ppermute(v, 'fsdp', [(i, i ^ d) for i in range(4)])  29.3 us
    ppermute x12, starting transfers between devices, to_z(): return lax.ppermute(v, 'patch', [(i, i ^ d) for i in range(4)])  15.8 us
    pallas_call x2, Pallas kernels, run_attend(): pl.pallas_call(attend_kernel, grid_spec=pltpu.PrefetchScalarGridSpec(num_...  15 us
    ppermute x21, starting transfers between devices, to_f(): return lax.ppermute(v, 'fsdp', [(i, i ^ d) for i in range(4)])  14.8 us
    pallas_call x4, Pallas kernels, run_project(): pl.pallas_call(project_kernel, grid=(3,), in_specs=[vmem] * 2 + [pl.Block...  10.1 us
    ppermute x2, waiting for transfers between devices, to_y(): return lax.ppermute(v, 'rep', [(0, 1), (1, 0)])  9.91 us
    pallas_call x2, Pallas kernels, run_norm(): pl.pallas_call(functools.partial(norm_kernel, s), in_specs=[pl.BlockSpec(...  6.22 us
  transfers between devices with their start and end apart: 35, of which 18 were waited for; matrix products, arithmetic and copies ran while one was open for 2% of the time, Pallas kernels for 14%

profile of v2, /device:TPU:0, one launch (start us, length us, event | category | flops | bytes accessed | tf_op | source)
XLA Modules:
  0.0 192.4 jit_solution(7047871524864636056)
XLA Ops:
  2.1 3.0 %collective-permute-start.3 = (bf16[384,1536]{1,0:T(8,128)(2,1)S(1)}, bf16[384,1536]{1,0:T(8,128)(2,1)S(1)}, u32[]{:S(2)}, u32[]{:S(2)}) collective-permute-start(bf16[384,1536]{1,0:T(8,128)(2,1)S(1)} %constant_dynamic-slice_fusion), channel_id=1, source_target_pairs={{0,8},{4,12},{8,0},{12,4},{1,9},{5,13},{9,1},{13,5},{2,10},{6,14},... | collective-permute-start | bytes 3538952 | tf_op jit(solution)/shard_map/ppermute | solution.py:387
  7.6 2.6 %collective-permute-start.1 = (bf16[144,1536]{1,0:T(8,128)(2,1)S(1)}, bf16[144,1536]{1,0:T(8,128)(2,1)}, u32[]{:S(2)}, u32[]{:S(2)}) collective-permute-start(bf16[144,1536]{1,0:T(8,128)(2,1)S(1)} %get-tuple-element.35.refs_0_.refs_4_), channel_id=1, source_target_pairs={{0,2},{1,3},{2,0},{3,1},{4,6},{5,7},{6,4},{7,5},{8,10},{9,11},{10,... | collective-permute-start | bytes 1327112 | tf_op jit(solution)/shard_map/ppermute | solution.py:393
  11.0 16.1 %collective-permute-done.refs_1_.refs_5_ = bf16[144,1536]{1,0:T(8,128)(2,1)S(1)} collective-permute-done((bf16[144,1536]{1,0:T(8,128)(2,1)S(1)}, bf16[144,1536]{1,0:T(8,128)(2,1)S(1)}, u32[]{:S(2)}, u32[]{:S(2)}) %collective-permute-start) | collective-permute-done | bytes 442400 | tf_op jit(solution)/shard_map/ppermute | solution.py:393
  29.9 2.6 %collective-permute-start.11 = (bf16[128,1536]{1,0:T(8,128)(2,1)}, bf16[128,1536]{1,0:T(8,128)(2,1)}, u32[]{:S(2)}, u32[]{:S(2)}) collective-permute-start(bf16[128,1536]{1,0:T(8,128)(2,1)} %slice_bitcast_fusion.refs_0_), channel_id=1, source_target_pairs={{0,2},{1,3},{2,0},{3,1},{4,6},{5,7},{6,4},{7,5},{8,10},{9,11},{10,... | collective-permute-start | bytes 1179656 | tf_op jit(solution)/shard_map/ppermute | solution.py:393
  35.7 12.6 %collective-permute-done.11.refs_2_ = bf16[128,1536]{1,0:T(8,128)(2,1)} collective-permute-done((bf16[128,1536]{1,0:T(8,128)(2,1)}, bf16[128,1536]{1,0:T(8,128)(2,1)}, u32[]{:S(2)}, u32[]{:S(2)}) %collective-permute-start.11) | collective-permute-done | bytes 393248 | tf_op jit(solution)/shard_map/ppermute | solution.py:393
  49.9 6.1 %collective-permute-done.2.refs_3_.refs_7_ = bf16[144,1536]{1,0:T(8,128)(2,1)} collective-permute-done((bf16[144,1536]{1,0:T(8,128)(2,1)}, bf16[144,1536]{1,0:T(8,128)(2,1)}, u32[]{:S(2)}, u32[]{:S(2)}) %collective-permute-start.2) | collective-permute-done | bytes 442400 | tf_op jit(solution)/shard_map/ppermute | solution.py:393
  58.8 3.1 %norm.2 = (bf16[128,1536]{1,0:T(8,128)(2,1)S(1)}, bf16[128,1536]{1,0:T(8,128)(2,1)S(1)}, bf16[128,1536]{1,0:T(8,128)(2,1)S(1)}, bf16[128,1536]{1,0:T(8,128)(2,1)S(1)}) custom-call(s32[2]{0:T(128)S(1)} %pad_add_fusion.key.at, bf16[144,1536]{1,0:T(8,128)(2,1)S(1)} %get-tuple-element.35.refs_0_.refs_4_, bf16[144,1536]{1,0:T(8,128)(2,1)S(1)} %copy-done.7, ...), custom_call_target="tpu_custom_call" | custom-call | flops 11796480 | bytes 3145728 | tf_op jit(solution)/shard_map/norm/pallas_call | solution.py:296
  65.0 3.2 %norm.3 = (bf16[128,1536]{1,0:T(8,128)(2,1)S(1)}, bf16[128,1536]{1,0:T(8,128)(2,1)S(1)}, bf16[128,1536]{1,0:T(8,128)(2,1)S(1)}, bf16[128,1536]{1,0:T(8,128)(2,1)S(1)}) custom-call(s32[2]{0:T(128)S(1)} %pad_add_fusion.key.at, bf16[128,1536]{1,0:T(8,128)(2,1)} %slice_bitcast_fusion.refs_0_, bf16[128,1536]{1,0:T(8,128)(2,1)} %collective-permute-done.10.refs_1_, ...), custom_call_target="tpu_custom_call" | custom-call | flops 11796480 | bytes 3145728 | tf_op jit(solution)/shard_map/norm/pallas_call | solution.py:296
  68.2 5.9 %collective-permute-done.6.second = bf16[128,1536]{1,0:T(8,128)(2,1)S(1)} collective-permute-done((bf16[128,1536]{1,0:T(8,128)(2,1)S(1)}, bf16[128,1536]{1,0:T(8,128)(2,1)S(1)}, u32[]{:S(2)}, u32[]{:S(2)}) %collective-permute-start.6) | collective-permute-done | bytes 393248 | tf_op jit(solution)/shard_map/ppermute | solution.py:387
  74.0 2.8 %collective-permute-done.8.second = bf16[128,1536]{1,0:T(8,128)(2,1)S(1)} collective-permute-done((bf16[128,1536]{1,0:T(8,128)(2,1)S(1)}, bf16[128,1536]{1,0:T(8,128)(2,1)S(1)}, u32[]{:S(2)}, u32[]{:S(2)}) %collective-permute-start.8) | collective-permute-done | bytes 393248 | tf_op jit(solution)/shard_map/ppermute | solution.py:387
  76.9 3.0 %copy-done = bf16[1536,3,768]{2,0,1:T(8,128)(2,1)S(1)} copy-done((bf16[1536,3,768]{2,0,1:T(8,128)(2,1)S(1)}, bf16[1536,3,768]{2,0,1:T(8,128)(2,1)}, u32[]{:S(2)}) %copy-start) | copy-done | bytes 7077912
  87.4 2.5 %project.4.kept = f32[2,128,2304]{2,1,0:T(8,128)S(1)} custom-call(bf16[128,1536]{1,0:T(8,128)(2,1)S(1)} %get-tuple-element.36.first, bf16[128,1536]{1,0:T(8,128)(2,1)S(1)} %collective-permute-done.6.second, bf16[3,1536,768]{2,1,0:T(8,128)(2,1)S(1)} %bitcast.44), custom_call_target="tpu_custom_call" | custom-call | flops 1811939328 | bytes 9437184 | tf_op jit(solution)/shard_map/project/pallas_call | solution.py:314
  90.1 9.9 %collective-permute-done.20.o_xb = bf16[192,1536]{1,0:T(8,128)(2,1)S(1)} collective-permute-done((bf16[192,1536]{1,0:T(8,128)(2,1)S(1)}, bf16[192,1536]{1,0:T(8,128)(2,1)S(1)}, u32[]{:S(2)}, u32[]{:S(2)}) %collective-permute-start.20) | collective-permute-done | bytes 589856 | tf_op jit(solution)/shard_map/ppermute | solution.py:390
  100.0 4.7 %collective-permute-done.29.second = bf16[128,1536]{1,0:T(8,128)(2,1)S(1)} collective-permute-done((bf16[128,1536]{1,0:T(8,128)(2,1)S(1)}, bf16[128,1536]{1,0:T(8,128)(2,1)S(1)}, u32[]{:S(2)}, u32[]{:S(2)}) %collective-permute-start.29) | collective-permute-done | bytes 393248 | tf_op jit(solution)/shard_map/ppermute | solution.py:387
  104.7 2.5 %project.7 = f32[2,128,2304]{2,1,0:T(8,128)S(1)} custom-call(bf16[128,1536]{1,0:T(8,128)(2,1)S(1)} %collective-permute-done.28.first, bf16[128,1536]{1,0:T(8,128)(2,1)S(1)} %collective-permute-done.29.second, bf16[3,1536,768]{2,1,0:T(8,128)(2,1)S(1)} %bitcast.45), custom_call_target="tpu_custom_call" | custom-call | flops 1811939328 | bytes 9437184 | tf_op jit(solution)/shard_map/project/pallas_call | solution.py:314
  109.1 4.3 %collective-permute-done.15.k_pair = bf16[2,128,768]{2,1,0:T(8,128)(2,1)S(1)} collective-permute-done((bf16[2,128,768]{2,1,0:T(8,128)(2,1)}, bf16[2,128,768]{2,1,0:T(8,128)(2,1)S(1)}, u32[]{:S(2)}, u32[]{:S(2)}) %collective-permute-start.15) | collective-permute-done | bytes 393248 | tf_op jit(solution)/shard_map/ppermute | solution.py:387
  115.1 2.5 %project.6.kept = f32[2,128,2304]{2,1,0:T(8,128)S(1)} custom-call(bf16[128,1536]{1,0:T(8,128)(2,1)S(1)} %get-tuple-element.45.first, bf16[128,1536]{1,0:T(8,128)(2,1)S(1)} %collective-permute-done.27.second, bf16[3,1536,768]{2,1,0:T(8,128)(2,1)S(1)} %bitcast.46), custom_call_target="tpu_custom_call" | custom-call | flops 1811939328 | bytes 9437184 | tf_op jit(solution)/shard_map/project/pallas_call | solution.py:314
  118.3 6.0 %collective-permute-done.14.over = bf16[128,2304]{1,0:T(8,128)(2,1)S(1)} collective-permute-done((bf16[128,2304]{1,0:T(8,128)(2,1)S(1)}, bf16[128,2304]{1,0:T(8,128)(2,1)S(1)}, u32[]{:S(2)}, u32[]{:S(2)}) %collective-permute-start.14) | collective-permute-done | bytes 589856 | tf_op jit(solution)/shard_map/ppermute | solution.py:387
  127.2 7.4 %attend.2 = (bf16[128,768]{1,0:T(8,128)(2,1)S(1)}, bf16[128,768]{1,0:T(8,128)(2,1)S(1)}, bf16[2,128,1536]{2,1,0:T(8,128)(2,1)S(1)}, bf16[128,1536]{1,0:T(8,128)(2,1)S(1)}, bf16[128,1536]{1,0:T(8,128)(2,1)S(1)}) custom-call(s32[2]{0:T(128)S(1)} %pad_add_fusion.key.at, f32[2,128,2304]{2,1,0:T(8,128)S(1)} %project.4.kept, ...), custom_call_target="tpu_custom_call" | custom-call | flops 1409286144 | bytes 14155776 | tf_op jit(solution)/shard_map/attend/pallas_call | solution.py:340
  136.7 3.5 %collective-permute-done.31.over = bf16[128,2304]{1,0:T(8,128)(2,1)S(1)} collective-permute-done((bf16[128,2304]{1,0:T(8,128)(2,1)S(1)}, bf16[128,2304]{1,0:T(8,128)(2,1)S(1)}, u32[]{:S(2)}, u32[]{:S(2)}) %collective-permute-start.31) | collective-permute-done | bytes 589856 | tf_op jit(solution)/shard_map/ppermute | solution.py:387
  140.2 7.6 %attend.3 = (bf16[128,768]{1,0:T(8,128)(2,1)S(1)}, bf16[128,768]{1,0:T(8,128)(2,1)S(1)}, bf16[2,128,1536]{2,1,0:T(8,128)(2,1)S(1)}, bf16[128,1536]{1,0:T(8,128)(2,1)S(1)}, bf16[128,1536]{1,0:T(8,128)(2,1)S(1)}) custom-call(s32[2]{0:T(128)S(1)} %pad_add_fusion.key.at, f32[2,128,2304]{2,1,0:T(8,128)S(1)} %project.6.kept, ...), custom_call_target="tpu_custom_call" | custom-call | flops 1409286144 | bytes 14155776 | tf_op jit(solution)/shard_map/attend/pallas_call | solution.py:340
  152.4 19.5 %collective-permute-done.33 = bf16[128,1536]{1,0:T(8,128)(2,1)S(1)} collective-permute-done((bf16[128,1536]{1,0:T(8,128)(2,1)S(1)}, bf16[128,1536]{1,0:T(8,128)(2,1)S(1)}, u32[]{:S(2)}, u32[]{:S(2)}) %collective-permute-start.33) | collective-permute-done | bytes 393248 | tf_op jit(solution)/shard_map/ppermute | solution.py:393
  173.8 13.0 %collective-permute-done.32 = bf16[128,1536]{1,0:T(8,128)(2,1)S(1)} collective-permute-done((bf16[128,1536]{1,0:T(8,128)(2,1)S(1)}, bf16[128,1536]{1,0:T(8,128)(2,1)S(1)}, u32[]{:S(2)}, u32[]{:S(2)}) %collective-permute-start.32) | collective-permute-done | bytes 393248 | tf_op jit(solution)/shard_map/ppermute | solution.py:393
  186.8 4.2 %collective-permute-done.34 = bf16[128,1536]{1,0:T(8,128)(2,1)S(1)} collective-permute-done((bf16[128,1536]{1,0:T(8,128)(2,1)S(1)}, bf16[128,1536]{1,0:T(8,128)(2,1)S(1)}, u32[]{:S(2)}, u32[]{:S(2)}) %collective-permute-start.34) | collective-permute-done | bytes 393248 | tf_op jit(solution)/shard_map/ppermute | solution.py:393
  (107 shorter events, 43.0 us)
Async XLA Ops:
  2.1 30.4 %collective-permute-start.3 = (bf16[384,1536]{1,0:T(8,128)(2,1)S(1)}, bf16[384,1536]{1,0:T(8,128)(2,1)S(1)}, u32[]{:S(2)}, u32[]{:S(2)}) collective-permute-start(bf16[384,1536]{1,0:T(8,128)(2,1)S(1)} %constant_dynamic-slice_fusion), channel_id=1, source_target_pairs={{0,8},{4,12},{8,0},{12,4},{1,9},{5,13},{9,1},{13,5},{2,10},{6,14},... | collective-permute-start | bytes 3538952 | tf_op jit(solution)/shard_map/ppermute | solution.py:387
  6.0 21.1 %collective-permute-start = (bf16[144,1536]{1,0:T(8,128)(2,1)S(1)}, bf16[144,1536]{1,0:T(8,128)(2,1)S(1)}, u32[]{:S(2)}, u32[]{:S(2)}) collective-permute-start(bf16[144,1536]{1,0:T(8,128)(2,1)S(1)} %get-tuple-element.35.refs_0_.refs_4_), channel_id=1, source_target_pairs={{0,1},{1,0},{2,3},{3,2},{4,5},{5,4},{6,7},{7,6},{8,9},{9,8},{10,11... | collective-permute-start | bytes 1327112 | tf_op jit(solution)/shard_map/ppermute | solution.py:393
  7.6 21.9 %collective-permute-start.1 = (bf16[144,1536]{1,0:T(8,128)(2,1)S(1)}, bf16[144,1536]{1,0:T(8,128)(2,1)}, u32[]{:S(2)}, u32[]{:S(2)}) collective-permute-start(bf16[144,1536]{1,0:T(8,128)(2,1)S(1)} %get-tuple-element.35.refs_0_.refs_4_), channel_id=1, source_target_pairs={{0,2},{1,3},{2,0},{3,1},{4,6},{5,7},{6,4},{7,5},{8,10},{9,11},{10,... | collective-permute-start | bytes 1327112 | tf_op jit(solution)/shard_map/ppermute | solution.py:393
  29.5 33.0 %collective-permute-start.10 = (bf16[128,1536]{1,0:T(8,128)(2,1)}, bf16[128,1536]{1,0:T(8,128)(2,1)}, u32[]{:S(2)}, u32[]{:S(2)}) collective-permute-start(bf16[128,1536]{1,0:T(8,128)(2,1)} %slice_bitcast_fusion.refs_0_), channel_id=1, source_target_pairs={{0,1},{1,0},{2,3},{3,2},{4,5},{5,4},{6,7},{7,6},{8,9},{9,8},{10,11... | collective-permute-start | bytes 1179656 | tf_op jit(solution)/shard_map/ppermute | solution.py:393
  29.9 18.4 %collective-permute-start.11 = (bf16[128,1536]{1,0:T(8,128)(2,1)}, bf16[128,1536]{1,0:T(8,128)(2,1)}, u32[]{:S(2)}, u32[]{:S(2)}) collective-permute-start(bf16[128,1536]{1,0:T(8,128)(2,1)} %slice_bitcast_fusion.refs_0_), channel_id=1, source_target_pairs={{0,2},{1,3},{2,0},{3,1},{4,6},{5,7},{6,4},{7,5},{8,10},{9,11},{10,... | collective-permute-start | bytes 1179656 | tf_op jit(solution)/shard_map/ppermute | solution.py:393
  32.5 23.5 %collective-permute-start.2 = (bf16[144,1536]{1,0:T(8,128)(2,1)}, bf16[144,1536]{1,0:T(8,128)(2,1)}, u32[]{:S(2)}, u32[]{:S(2)}) collective-permute-start(bf16[144,1536]{1,0:T(8,128)(2,1)} %collective-permute-done.1.refs_2_.refs_6_), channel_id=1, source_target_pairs={{0,1},{1,0},{2,3},{3,2},{4,5},{5,4},{6,7},{7,6},{8,9},{9,8},{10,11... | collective-permute-start | bytes 1327112 | tf_op jit(solution)/shard_map/ppermute | solution.py:393
  32.5 29.4 %collective-permute-start.4 = (bf16[2,128,768]{2,1,0:T(8,128)(2,1)}, bf16[2,128,768]{2,1,0:T(8,128)(2,1)}, u32[]{:S(2)}, u32[]{:S(2)}) collective-permute-start(bf16[2,128,768]{2,1,0:T(8,128)(2,1)} %param.18), channel_id=1, source_target_pairs={{0,8},{4,12},{8,0},{12,4},{1,9},{5,13},{9,1},{13,5},{2,10},{6,14},... | collective-permute-start | bytes 1179656 | tf_op jit(solution)/shard_map/ppermute | solution.py:387
  33.1 28.8 %collective-permute-start.5 = (bf16[2,128,768]{2,1,0:T(8,128)(2,1)}, bf16[2,128,768]{2,1,0:T(8,128)(2,1)}, u32[]{:S(2)}, u32[]{:S(2)}) collective-permute-start(bf16[2,128,768]{2,1,0:T(8,128)(2,1)} %param.19), channel_id=1, source_target_pairs={{0,8},{4,12},{8,0},{12,4},{1,9},{5,13},{9,1},{13,5},{2,10},{6,14},... | collective-permute-start | bytes 1179656 | tf_op jit(solution)/shard_map/ppermute | solution.py:387
  48.3 19.8 %collective-permute-start.9 = (bf16[192,1536]{1,0:T(8,128)(2,1)}, bf16[192,1536]{1,0:T(8,128)(2,1)}, u32[]{:S(2)}, u32[]{:S(2)}) collective-permute-start(bf16[192,1536]{1,0:T(8,128)(2,1)} %get-tuple-element.67), channel_id=1, source_target_pairs={{0,16},{16,0},{1,17},{17,1},{2,18},{18,2},{3,19},{19,3},{4,20},{20... | collective-permute-start | bytes 1769480 | tf_op jit(solution)/shard_map/ppermute | solution.py:390
  62.5 14.3 %collective-permute-start.8 = (bf16[128,1536]{1,0:T(8,128)(2,1)S(1)}, bf16[128,1536]{1,0:T(8,128)(2,1)S(1)}, u32[]{:S(2)}, u32[]{:S(2)}) collective-permute-start(bf16[128,1536]{1,0:T(8,128)(2,1)S(1)} %get-tuple-element.43), channel_id=1, source_target_pairs={{0,12},{4,8},{8,4},{12,0},{1,13},{5,9},{9,5},{13,1},{2,14},{6,10},... | collective-permute-start | bytes 1179656 | tf_op jit(solution)/shard_map/ppermute | solution.py:387
  62.5 14.3 %collective-permute-start.7 = (bf16[128,1536]{1,0:T(8,128)(2,1)S(1)}, bf16[128,1536]{1,0:T(8,128)(2,1)S(1)}, u32[]{:S(2)}, u32[]{:S(2)}) collective-permute-start(bf16[128,1536]{1,0:T(8,128)(2,1)S(1)} %get-tuple-element.41), channel_id=1, source_target_pairs={{0,4},{4,0},{8,12},{12,8},{1,5},{5,1},{9,13},{13,9},{2,6},{6,2},{1... | collective-permute-start | bytes 1179656 | tf_op jit(solution)/shard_map/ppermute | solution.py:387
  84.3 20.4 %collective-permute-start.28 = (bf16[128,1536]{1,0:T(8,128)(2,1)S(1)}, bf16[128,1536]{1,0:T(8,128)(2,1)S(1)}, u32[]{:S(2)}, u32[]{:S(2)}) collective-permute-start(bf16[128,1536]{1,0:T(8,128)(2,1)S(1)} %get-tuple-element.53), channel_id=1, source_target_pairs={{0,4},{4,0},{8,12},{12,8},{1,5},{5,1},{9,13},{13,9},{2,6},{6,2},{1... | collective-permute-start | bytes 1179656 | tf_op jit(solution)/shard_map/ppermute | solution.py:387
  84.3 15.7 %collective-permute-start.20 = (bf16[192,1536]{1,0:T(8,128)(2,1)S(1)}, bf16[192,1536]{1,0:T(8,128)(2,1)S(1)}, u32[]{:S(2)}, u32[]{:S(2)}) collective-permute-start(bf16[192,1536]{1,0:T(8,128)(2,1)S(1)} %copy-done.10), channel_id=1, source_target_pairs={{0,16},{16,0},{1,17},{17,1},{2,18},{18,2},{3,19},{19,3},{4,20},{20... | collective-permute-start | bytes 1769480 | tf_op jit(solution)/shard_map/ppermute | solution.py:390
  85.9 14.2 %collective-permute-start.27 = (bf16[128,1536]{1,0:T(8,128)(2,1)S(1)}, bf16[128,1536]{1,0:T(8,128)(2,1)S(1)}, u32[]{:S(2)}, u32[]{:S(2)}) collective-permute-start(bf16[128,1536]{1,0:T(8,128)(2,1)S(1)} %get-tuple-element.52), channel_id=1, source_target_pairs={{0,8},{4,12},{8,0},{12,4},{1,9},{5,13},{9,1},{13,5},{2,10},{6,14},... | collective-permute-start | bytes 1179656 | tf_op jit(solution)/shard_map/ppermute | solution.py:387
  86.4 18.3 %collective-permute-start.29 = (bf16[128,1536]{1,0:T(8,128)(2,1)S(1)}, bf16[128,1536]{1,0:T(8,128)(2,1)S(1)}, u32[]{:S(2)}, u32[]{:S(2)}) collective-permute-start(bf16[128,1536]{1,0:T(8,128)(2,1)S(1)} %get-tuple-element.55), channel_id=1, source_target_pairs={{0,12},{4,8},{8,4},{12,0},{1,13},{5,9},{9,5},{13,1},{2,14},{6,10},... | collective-permute-start | bytes 1179656 | tf_op jit(solution)/shard_map/ppermute | solution.py:387
  107.2 17.0 %collective-permute-start.30 = (f32[2,128,2304]{2,1,0:T(8,128)S(1)}, f32[2,128,2304]{2,1,0:T(8,128)S(1)}, u32[]{:S(2)}, u32[]{:S(2)}) collective-permute-start(f32[2,128,2304]{2,1,0:T(8,128)S(1)} %project.7), channel_id=1, source_target_pairs={{0,4},{4,0},{8,12},{12,8},{1,5},{5,1},{9,13},{13,9},{2,6},{6,2},{1... | collective-permute-start | bytes 7077896 | tf_op jit(solution)/shard_map/ppermute | solution.py:387
  107.9 17.6 %collective-permute-start.19 = (bf16[768,1536]{1,0:T(8,128)(2,1)S(1)}, bf16[768,1536]{1,0:T(8,128)(2,1)S(1)}, u32[]{:S(2)}, u32[]{:S(2)}) collective-permute-start(bf16[768,1536]{1,0:T(8,128)(2,1)S(1)} %copy-done.1), channel_id=1, source_target_pairs={{0,4},{4,0},{8,12},{12,8},{1,5},{5,1},{9,13},{13,9},{2,6},{6,2},{1... | collective-permute-start | bytes 7077896 | tf_op jit(solution)/shard_map/ppermute | solution.py:387
  108.5 15.7 %collective-permute-start.14 = (bf16[128,2304]{1,0:T(8,128)(2,1)S(1)}, bf16[128,2304]{1,0:T(8,128)(2,1)S(1)}, u32[]{:S(2)}, u32[]{:S(2)}) collective-permute-start(bf16[128,2304]{1,0:T(8,128)(2,1)S(1)} %fusion.12), channel_id=1, source_target_pairs={{0,8},{4,12},{8,0},{12,4},{1,9},{5,13},{9,1},{13,5},{2,10},{6,14},... | collective-permute-start | bytes 1769480 | tf_op jit(solution)/shard_map/ppermute | solution.py:387
  124.9 15.3 %collective-permute-start.31 = (bf16[128,2304]{1,0:T(8,128)(2,1)S(1)}, bf16[128,2304]{1,0:T(8,128)(2,1)S(1)}, u32[]{:S(2)}, u32[]{:S(2)}) collective-permute-start(bf16[128,2304]{1,0:T(8,128)(2,1)S(1)} %fusion.13), channel_id=1, source_target_pairs={{0,8},{4,12},{8,0},{12,4},{1,9},{5,13},{9,1},{13,5},{2,10},{6,14},... | collective-permute-start | bytes 1769480 | tf_op jit(solution)/shard_map/ppermute | solution.py:387
  135.0 38.8 %collective-permute-start.24 = (bf16[128,1536]{1,0:T(8,128)(2,1)S(1)}, bf16[128,1536]{1,0:T(8,128)(2,1)S(1)}, u32[]{:S(2)}, u32[]{:S(2)}) collective-permute-start(bf16[128,1536]{1,0:T(8,128)(2,1)S(1)} %get-tuple-element.49), channel_id=1, source_target_pairs={{0,1},{1,0},{2,3},{3,2},{4,5},{5,4},{6,7},{7,6},{8,9},{9,8},{10,11... | collective-permute-start | bytes 1179656 | tf_op jit(solution)/shard_map/ppermute | solution.py:393
  147.8 24.1 %collective-permute-start.33 = (bf16[128,1536]{1,0:T(8,128)(2,1)S(1)}, bf16[128,1536]{1,0:T(8,128)(2,1)S(1)}, u32[]{:S(2)}, u32[]{:S(2)}) collective-permute-start(bf16[128,1536]{1,0:T(8,128)(2,1)S(1)} %get-tuple-element.60), channel_id=1, source_target_pairs={{0,1},{1,0},{2,3},{3,2},{4,5},{5,4},{6,7},{7,6},{8,9},{9,8},{10,11... | collective-permute-start | bytes 1179656 | tf_op jit(solution)/shard_map/ppermute | solution.py:393
  148.2 25.6 %collective-permute-start.26 = (bf16[128,1536]{1,0:T(8,128)(2,1)S(1)}, bf16[128,1536]{1,0:T(8,128)(2,1)S(1)}, u32[]{:S(2)}, u32[]{:S(2)}) collective-permute-start(bf16[128,1536]{1,0:T(8,128)(2,1)S(1)} %fusion.7), channel_id=1, source_target_pairs={{0,2},{1,3},{2,0},{3,1},{4,6},{5,7},{6,4},{7,5},{8,10},{9,11},{10,... | collective-permute-start | bytes 1179656 | tf_op jit(solution)/shard_map/ppermute | solution.py:393
  150.6 36.2 %collective-permute-start.32 = (bf16[128,1536]{1,0:T(8,128)(2,1)S(1)}, bf16[128,1536]{1,0:T(8,128)(2,1)S(1)}, u32[]{:S(2)}, u32[]{:S(2)}) collective-permute-start(bf16[128,1536]{1,0:T(8,128)(2,1)S(1)} %get-tuple-element.59), channel_id=1, source_target_pairs={{0,1},{1,0},{2,3},{3,2},{4,5},{5,4},{6,7},{7,6},{8,9},{9,8},{10,11... | collective-permute-start | bytes 1179656 | tf_op jit(solution)/shard_map/ppermute | solution.py:393
  172.0 18.9 %collective-permute-start.34 = (bf16[128,1536]{1,0:T(8,128)(2,1)S(1)}, bf16[128,1536]{1,0:T(8,128)(2,1)S(1)}, u32[]{:S(2)}, u32[]{:S(2)}) collective-permute-start(bf16[128,1536]{1,0:T(8,128)(2,1)S(1)} %fusion.2), channel_id=1, source_target_pairs={{0,2},{1,3},{2,0},{3,1},{4,6},{5,7},{6,4},{7,5},{8,10},{9,11},{10,... | collective-permute-start | bytes 1179656 | tf_op jit(solution)/shard_map/ppermute | solution.py:393
  (27 other events, 286.7 us)

commit v3 on v2

--- a/solution.py
+++ b/solution.py
@@ -166,24 +166,26 @@
 
 
 def norm_kernel(s, key, *refs):
-    blocks, turns, outs, held = refs[:4], refs[4:8], refs[8:12], refs[12]
-    rows, feats = outs[0].shape
-    mean = sum(
-        jnp.sum(b[:rows].astype(jnp.float32), axis=-1, keepdims=True) for b in blocks
-    ) / (4 * feats)
+    blocks, turns, (mine, pair, far, held) = refs[:4], refs[4:8], refs[8:]
+    rows, feats = mine.shape
+
+    def block(r):
+        return blocks[r][:rows].astype(jnp.float32)
+
+    mean = sum(jnp.sum(block(r), axis=-1, keepdims=True) for r in range(4)) / (4 * feats)
     spread = sum(
-        jnp.sum(jnp.square(b[:rows].astype(jnp.float32) - mean), axis=-1, keepdims=True)
-        for b in blocks
+        jnp.sum(jnp.square(block(r) - mean), axis=-1, keepdims=True) for r in range(4)
     ) / (4 * feats)
     rate = lax.rsqrt(spread + EPS)
-    for r, (block, turn) in enumerate(zip(blocks, turns)):
-        low = turn[rows:].astype(jnp.float32)
+    for r, turn in enumerate(turns):
+        low = turn[rows : rows + 16].astype(jnp.float32)
         shift = low[2 * s : 2 * s + 1]
         scale = low[2 * s + 1 : 2 * s + 2]
-        centered = block[:rows].astype(jnp.float32) - mean
-        held[r ^ key[0]] = (centered * rate * (1.0 + scale) + shift).astype(jnp.bfloat16)
-    for j in range(4):
-        outs[j][...] = held[j]
+        held[r ^ key[0]] = ((block(r) - mean) * rate * (1.0 + scale) + shift).astype(jnp.bfloat16)
+    mine[...] = held[0]
+    pair[...] = held[1]
+    far[:rows] = held[2]
+    far[rows:] = held[3]
 
 
 def project_kernel(first, second, weight, out, held):
@@ -201,7 +203,7 @@
 
 def attend_kernel(
     at, kept, back, over, k_pair, v_pair, k_x, v_x, k_d, v_d, tables, gains,
-    o_own, o_pair, o_x, o_xa, o_xb, o_d, o_da, o_db,
+    o_own, o_pair, o_x, o_y, o_d, o_dy,
     keys_out, values_out, near, far_one, far_three, mixed, held, columns, sems,
 ):
     rows, width = keys_out.shape
@@ -211,15 +213,18 @@
     lane = lax.broadcasted_iota(jnp.int32, (rows, size), 1)
     low = (lane // (size // 4)) % 2 == 0
     rep = at[1]
-    copies = []
-    for j, refs in enumerate(((o_own,), (o_pair,), (o_x, o_xa, o_xb), (o_d, o_da, o_db))):
-        start = 0
-        for ref in refs:
-            part = columns.at[j, start : start + ref.shape[0]]
-            copy = pltpu.make_async_copy(ref, part, sems.at[len(copies)])
-            copy.start()
-            copies.append(copy)
-            start += ref.shape[0]
+    moves = [(o_own, columns.at[0]), (o_pair, columns.at[1])]
+    for j, low_half, high_half in ((2, o_x, o_y), (3, o_d, o_dy)):
+        for ref, first in ((low_half, 0), (high_half, half)):
+            start = ref.shape[0] - 2 * half
+            for k in range(2):
+                part = columns.at[j, first : first + half, k * width : (k + 1) * width]
+                moves.append((ref.at[start + k * half : start + (k + 1) * half], part))
+    copies = [
+        pltpu.make_async_copy(ref, part, sems.at[n]) for n, (ref, part) in enumerate(moves)
+    ]
+    for copy in copies:
+        copy.start()
 
     def summed(first):
         cols = slice(first, first + size)
@@ -239,8 +244,8 @@
         value = summed(2 * width + h * size).astype(jnp.bfloat16)
         keys_out[:, cols] = key
         values_out[:, cols] = value
-        keys = jnp.concatenate([key] + [s[0, :, cols] for s in (k_pair, k_x, k_d)], axis=0)
-        seen = jnp.concatenate([value] + [s[0, :, cols] for s in (v_pair, v_x, v_d)], axis=0)
+        keys = jnp.concatenate([key] + [s[:, cols] for s in (k_pair, k_x, k_d)], axis=0)
+        seen = jnp.concatenate([value] + [s[:, cols] for s in (v_pair, v_x, v_d)], axis=0)
         scores = (
             lax.dot_general(
                 query, keys, (((1,), (1,)), ((), ())), preferred_element_type=jnp.float32
@@ -266,6 +271,28 @@
     near[1] = held[2]
     far_one[...] = held[1]
     far_three[...] = held[3]
+
+
+TIES = {'kept1': ('cross_far',),
+ 'last1': ('rest0',),
+ 'late': ('two0',),
+ 'sent0': ('three1', 'o_pair', 's_pair'),
+ 'sent0_last': (),
+ 'sent1_last': (),
+ 'use1': ('kept0',)}
+WORK = {'attend0': 6,
+ 'attend1': 9,
+ 'kept0': 9,
+ 'kept1': 11,
+ 'norm0': 8,
+ 'norm1': 9,
+ 'second': 10,
+ 'sent0': 9,
+ 'sent1': 9}
+
+
+def cost(name):
+    return pl.CostEstimate(flops=10 ** WORK[name], bytes_accessed=10**6, transcendentals=0)
 
 
 def params(mebibytes):
@@ -288,26 +315,41 @@
     )(timestep, latent, modulation.transpose(1, 0, 2))
 
 
-def run_norm(s, key, blocks, turns):
-    rows = blocks[-1].shape[0] if s else blocks[-1].shape[0] - 16
+def second_kernel(latent, out):
+    out[...] = latent[0]
+
+
+def run_second(latent):
+    _, rows, feats = latent.shape
+    return pl.pallas_call(
+        second_kernel,
+        grid=(1,),
+        in_specs=[pl.BlockSpec((1, rows, feats), lambda i: (1, 0, 0))],
+        out_specs=pl.BlockSpec((rows, feats), lambda i: (0, 0)),
+        out_shape=jax.ShapeDtypeStruct((rows, feats), jnp.bfloat16),
+        compiler_params=params(16),
+        cost_estimate=cost("second"),
+        name="second",
+    )(latent)
+
+
+def run_norm(s, key, rows, blocks, turns):
     cols = blocks[0].shape[1]
     vmem = pl.BlockSpec(memory_space=pltpu.VMEM)
     shape = jax.ShapeDtypeStruct((rows, cols), jnp.bfloat16)
     return pl.pallas_call(
         functools.partial(norm_kernel, s),
         in_specs=[pl.BlockSpec(memory_space=pltpu.SMEM)] + [vmem] * 8,
-        out_specs=[vmem] * 4,
-        out_shape=[shape] * 4,
+        out_specs=[vmem] * 3,
+        out_shape=[shape, shape, jax.ShapeDtypeStruct((2 * rows, cols), jnp.bfloat16)],
         scratch_shapes=[pltpu.VMEM((4, rows, cols), jnp.bfloat16)],
         compiler_params=params(16),
-        cost_estimate=pl.CostEstimate(
-            flops=60 * rows * cols, bytes_accessed=16 * rows * cols, transcendentals=0
-        ),
+        cost_estimate=cost(f"norm{s}"),
         name="norm",
     )(key, *blocks, *turns)
 
 
-def run_project(first, second, weight):
+def run_project(name, first, second, weight):
     rows, depth = first.shape
     wide = weight.shape[2]
     vmem = pl.BlockSpec((rows, depth), lambda i: (0, 0))
@@ -319,11 +361,7 @@
         out_shape=jax.ShapeDtypeStruct((2, rows, 3 * wide), jnp.float32),
         scratch_shapes=[pltpu.VMEM((2 * rows, depth), jnp.bfloat16)],
         compiler_params=params(24),
-        cost_estimate=pl.CostEstimate(
-            flops=12 * rows * depth * wide,
-            bytes_accessed=6 * depth * wide + 24 * rows * wide,
-            transcendentals=0,
-        ),
+        cost_estimate=cost(name),
         name="project",
     )(first, second, weight)
 
@@ -334,7 +372,11 @@
     feats = columns[0].shape[1]
     full = pl.BlockSpec(memory_space=pltpu.VMEM)
     first = pl.BlockSpec((1, rows, triple), lambda i, at: (0, 0, 0))
-    seen = pl.BlockSpec((1, rows, width), lambda i, at: (s, 0, 0))
+    samples = 2
+    seen = [
+        pl.BlockSpec((rows, width), lambda i, at: (s, 0)),
+        pl.BlockSpec((rows, width), lambda i, at: (samples + s, 0)),
+    ]
     head = jax.ShapeDtypeStruct((rows, width), jnp.bfloat16)
     term = jax.ShapeDtypeStruct((rows, feats), jnp.bfloat16)
     return pl.pallas_call(
@@ -343,26 +385,22 @@
             num_scalar_prefetch=1,
             grid=(1,),
             in_specs=[first, first, full]
-            + [seen] * 6
+            + seen * 3
             + [full] * 2
-            + [pl.BlockSpec(memory_space=pl.ANY)] * 8,
+            + [pl.BlockSpec(memory_space=pl.ANY)] * 6,
             out_specs=[full] * 5,
             scratch_shapes=[
                 pltpu.VMEM((2, rows, width // 2), jnp.bfloat16),
                 pltpu.VMEM((4, rows, feats), jnp.bfloat16),
                 pltpu.VMEM((4, width, feats), jnp.bfloat16),
-                pltpu.SemaphoreType.DMA((8,)),
+                pltpu.SemaphoreType.DMA((10,)),
             ],
         ),
         out_shape=[head, head, jax.ShapeDtypeStruct((2, rows, feats), jnp.bfloat16), term, term],
         compiler_params=params(28),
-        cost_estimate=pl.CostEstimate(
-            flops=8 * rows * width * feats + 16 * rows * rows * width,
-            bytes_accessed=8 * width * feats + 16 * rows * triple,
-            transcendentals=0,
-        ),
+        cost_estimate=cost(f"attend{s}"),
         name="attend",
-    )(at, kept, back, over, *stale, tables, gains, *columns)
+    )(at, kept, back, over, *[v for v in stale for _ in range(2)], tables, gains, *columns)
 
 
 def shards_four(
@@ -395,25 +433,15 @@
     def after(v, *deps):
         return lax.optimization_barrier((v, *deps))[0]
 
-    packed, gate = run_pack(timestep, latent, modulation)
-    own = [packed, latent[1]]
-    two, one, three = [], [], []
-    for s in range(samples):
-        start = own[s] if s == 0 else after(own[s], one[-1], two[-1])
-        two.append(to_z(start, 2))
-        one.append(to_z(start, 1))
-        three.append(to_z(two[s], 1))
-    turns = (own[0], one[0], two[0], three[0])
-
-    deep = out_weight.shape[0] // 2
-    o_half = lax.dynamic_slice_in_dim(out_weight, y * deep, deep, 0)
-    o_x = to_f(o_half, 2)
-    k_x, v_x = to_f(after(stale_keys, o_x), 2), to_f(after(stale_values, o_x), 2)
-    o_xa = to_y(o_x[: deep // 2])
-    o_xb = to_y(after(o_x[deep // 2 :], o_xa))
-    over_x = (o_x, o_xa, o_xb)
-    columns = (out_weight, to_f(out_weight, 1), *over_x, *[to_f(v, 1) for v in over_x])
-    stale_seen = (to_f(stale_keys, 1), to_f(stale_values, 1), k_x, v_x, to_f(k_x, 1), to_f(v_x, 1))
+    made = {}
+
+    def make(name, value):
+        made[name] = value
+        return value
+
+    def tie(name, value):
+        deps = [made[dep] for dep in TIES.get(name, ())]
+        return after(value, *deps) if deps else value
 
     quarter = size // 4
     freq = 10000.0 ** (-jnp.arange(quarter, dtype=jnp.float32) / quarter)
@@ -432,37 +460,68 @@
     at = jnp.stack([key, y]).astype(jnp.int32)
 
     weight = qkv_weight.transpose(1, 0, 2)
-    fence = (k_x, v_x)
-    shared, normed = [], []
+    packed, gate = run_pack(timestep, latent, modulation)
+    make("packed", packed)
+    two, one, three = [make("two0", to_z(packed, 2))], [make("one0", to_z(packed, 1))], []
+    three.append(make("three0", to_z(two[0], 1)))
+    deep = out_weight.shape[0] // 2
+    width = stale_keys.shape[2]
+    o_half = lax.dynamic_slice_in_dim(out_weight, y * deep, deep, 0)
+    stale = [v.reshape(samples * rows, width) for v in (stale_keys, stale_values)]
+    cut = len(stale) * samples * rows
+    far = jnp.concatenate([*stale, o_half[:, :width], o_half[:, width:]])
+    far = make("far", to_f(tie("far", far), 2))
+    late = run_second(tie("late", latent))
+    two.append(make("two1", to_z(late, 2)))
+    one.append(make("one1", to_z(tie("one1", late), 1)))
+    three.append(make("three1", to_z(two[1], 1)))
+    turns = (packed, one[0], two[0], three[0])
+    blocks = (turns, (late, one[1], two[1], three[1]))
+
+    shared = []
     for s in range(samples):
-        modded = run_norm(s, at, (own[s], one[s], two[s], three[s]), turns)
-        over = to_f(after(modded[2], *fence), 2)
-        cross = to_f(after(modded[3], *fence), 3)
-        fence = (over, cross)
-        normed.append(modded[0])
-        shared.append((modded[0], to_f(modded[1], 1), over, cross))
+        last = tie(f"norm{s}", blocks[s][3])
+        mine, pair, away = run_norm(s, at, rows, (*blocks[s][:3], last), turns)
+        make(f"mine{s}", mine)
+        away = make(f"away{s}", to_f(tie(f"away{s}", away), 2))
+        pair = make(f"pair{s}", to_f(tie(f"pair{s}", pair), 1))
+        shared.append((mine, pair, away))
+    o_y = make("o_y", to_y(tie("o_y", far[cut:])))
+    o_pair = make("o_pair", to_f(tie("o_pair", out_weight), 1))
+    s_pair = make("s_pair", to_f(tie("s_pair", jnp.concatenate(stale)), 1))
+    cross_far = make("cross_far", to_f(tie("cross_far", far), 1))
     halves, turned = [], []
     for s in range(samples):
-        mine, pair, over, cross = shared[s]
-        cross = after(cross, over, o_xa, *normed) if s == 0 else after(cross, over, o_xb, part)
-        sent = run_project(pair, cross, weight)
-        back = to_f(sent, 1)
-        kept = run_project(mine, over, weight)
-        part = (kept[1] + back[1]).astype(jnp.bfloat16)
+        mine, pair, away = shared[s]
+        away = tie(f"use{s}", away)
+        over, cross = away[:rows], make(f"cross{s}", to_f(away[rows:], 1))
+        if s == 1:
+            cross_y = make("cross_y", to_f(tie("cross_y", o_y), 1))
+        if f"sent{s}_last" in TIES:
+            kept = make(f"kept{s}", run_project(f"kept{s}", tie(f"kept{s}", mine), over, weight))
+            sent = run_project(f"sent{s}", pair, tie(f"sent{s}", cross), weight)
+        else:
+            sent = run_project(f"sent{s}", pair, tie(f"sent{s}", cross), weight)
+            kept = make(f"kept{s}", run_project(f"kept{s}", tie(f"kept{s}", mine), over, weight))
+        back = make(f"back{s}", to_f(sent, 1))
+        part = make(f"part{s}", (kept[1] + back[1]).astype(jnp.bfloat16))
         halves.append((kept, back))
-        turned.append(to_f(after(part, *turned), 2))
+        turned.append(make(f"turned{s}", to_f(tie(f"turned{s}", part), 2)))
+    columns = (out_weight, o_pair, far, o_y, cross_far, cross_y)
+    stale_seen = (s_pair, far, cross_far)
     keys, values, outs = [], [], []
     for s in range(samples):
         kept, back = halves[s]
         new_keys, new_values, near, far_one, far_three = run_attend(
-            s, at, kept, back, turned[s], stale_seen, tables, gains, columns
+            s, at, kept, back, tie(f"attend{s}", turned[s]), stale_seen, tables, gains, columns
         )
         keys.append(new_keys)
         values.append(new_values)
-        come = to_z(far_three, 1)
-        rest = to_z((near[1].astype(jnp.float32) + come.astype(jnp.float32)).astype(jnp.bfloat16), 2)
-        come = to_z(far_one, 1)
-        attended = (near[0].astype(jnp.float32) + come.astype(jnp.float32)) + rest.astype(jnp.float32)
+        come = make(f"come{s}", to_z(far_three, 1))
+        rest = near[1].astype(jnp.float32) + come.astype(jnp.float32)
+        rest = make(f"rest{s}", to_z(rest.astype(jnp.bfloat16), 2))
+        last = make(f"last{s}", to_z(tie(f"last{s}", far_one), 1))
+        attended = (near[0].astype(jnp.float32) + last.astype(jnp.float32)) + rest.astype(jnp.float32)
         outs.append((latent[s].astype(jnp.float32) + gate[s] * attended).astype(jnp.bfloat16))
     return (jnp.stack(outs), jnp.stack(keys), jnp.stack(values))
 

time: 193 us -> 182 us (0.943)
  local copies, waits for them, and re-layouts: 8.19 us -> 4.42 us
  Pallas kernels: 32.1 us -> 29.1 us
  waiting for transfers between devices: 113 us -> 110 us
  starting transfers between devices: 33.7 us -> 31.1 us
    ppermute x2 -> x1, waiting for transfers between devices: 9.91 us -> 0.48 us  [to_y(): return lax.ppermute(v, 'rep', [(0, 1), (1, 0)])]
    ppermute x21 -> x15, starting transfers between devices: 14.8 us -> 7.55 us  [to_f(): return lax.ppermute(v, 'fsdp', [(i, i ^ d) for i in range(4)])]
    ppermute x12, starting transfers between devices: 15.8 us -> 21.9 us  [to_z(): return lax.ppermute(v, 'patch', [(i, i ^ d) for i in range(4)])]
    ppermute x12, waiting for transfers between devices: 74 us -> 77.9 us  [to_z(): return lax.ppermute(v, 'patch', [(i, i ^ d) for i in range(4)])]
    pallas_call x2, Pallas kernels: 15 us -> 11.3 us  [run_attend(): pl.pallas_call(attend_kernel, grid_spec=pltpu.PrefetchScalarGridSpec(num_...]
    ppermute x21 -> x15, waiting for transfers between devices: 29.3 us -> 31.9 us  [to_f(): return lax.ppermute(v, 'fsdp', [(i, i ^ d) for i in range(4)])]
    unnamed x32, local copies, waits for them, and re-layouts: 4.85 us -> 2.89 us
  transfers between devices with their start and end apart: 35 -> 28, of which waited for: 18 -> 15; matrix products, arithmetic and copies ran while one was open for 2% -> 3% of each run, Pallas kernels for 14% -> 16%
where the time goes in v3:
time: 182 us
  waiting for transfers between devices  110 us (60%)
  starting transfers between devices  31.1 us (17%)
  Pallas kernels  29.1 us (16%)
  other arithmetic  5.77 us (3%)
  local copies, waits for them, and re-layouts  4.42 us (2%)
    ppermute x12, waiting for transfers between devices, to_z(): return lax.ppermute(v, 'patch', [(i, i ^ d) for i in range(4)])  77.9 us
    ppermute x15, waiting for transfers between devices, to_f(): return lax.ppermute(v, 'fsdp', [(i, i ^ d) for i in range(4)])  31.9 us
    ppermute x12, starting transfers between devices, to_z(): return lax.ppermute(v, 'patch', [(i, i ^ d) for i in range(4)])  21.9 us
    pallas_call x2, Pallas kernels, run_attend(): pl.pallas_call(attend_kernel, grid_spec=pltpu.PrefetchScalarGridSpec(num_...  11.3 us
    pallas_call x4, Pallas kernels, run_project(): pl.pallas_call(project_kernel, grid=(3,), in_specs=[vmem] * 2 + [pl.Block...  10.3 us
    ppermute x15, starting transfers between devices, to_f(): return lax.ppermute(v, 'fsdp', [(i, i ^ d) for i in range(4)])  7.55 us
    pallas_call x2, Pallas kernels, run_norm(): pl.pallas_call(functools.partial(norm_kernel, s), in_specs=[pl.BlockSpec(...  5.88 us
  transfers between devices with their start and end apart: 28, of which 15 were waited for; matrix products, arithmetic and copies ran while one was open for 3% of the time, Pallas kernels for 16%

profile of v3, /device:TPU:0, one launch (start us, length us, event | category | flops | bytes accessed | tf_op | source)
XLA Modules:
  0.0 181.6 jit_solution(7035174279216836553)
XLA Ops:
  4.3 4.1 %collective-permute-start.1 = (bf16[144,1536]{1,0:T(8,128)(2,1)S(1)}, bf16[144,1536]{1,0:T(8,128)(2,1)S(1)}, u32[]{:S(2)}, u32[]{:S(2)}) collective-permute-start(bf16[144,1536]{1,0:T(8,128)(2,1)S(1)} %get-tuple-element.27.refs_0_.refs_4_), channel_id=1, source_target_pairs={{0,2},{1,3},{2,0},{3,1},{4,6},{5,7},{6,4},{7,5},{8,10},{9,11},{10,... | collective-permute-start | bytes 1327112 | tf_op jit(solution)/shard_map/ppermute | solution.py:431
  14.3 13.9 %collective-permute-done.1.refs_2_.refs_6_ = bf16[144,1536]{1,0:T(8,128)(2,1)S(1)} collective-permute-done((bf16[144,1536]{1,0:T(8,128)(2,1)S(1)}, bf16[144,1536]{1,0:T(8,128)(2,1)S(1)}, u32[]{:S(2)}, u32[]{:S(2)}) %collective-permute-start.1) | collective-permute-done | bytes 442400 | tf_op jit(solution)/shard_map/ppermute | solution.py:431
  29.6 3.4 %collective-permute-start.6 = (bf16[128,1536]{1,0:T(8,128)(2,1)}, bf16[128,1536]{1,0:T(8,128)(2,1)}, u32[]{:S(2)}, u32[]{:S(2)}) collective-permute-start(bf16[128,1536]{1,0:T(8,128)(2,1)} %second.1.refs_0_), channel_id=1, source_target_pairs={{0,2},{1,3},{2,0},{3,1},{4,6},{5,7},{6,4},{7,5},{8,10},{9,11},{10,... | collective-permute-start | bytes 1179656 | tf_op jit(solution)/shard_map/ppermute | solution.py:431
  33.1 8.8 %collective-permute-done.refs_1_.refs_5_ = bf16[144,1536]{1,0:T(8,128)(2,1)S(1)} collective-permute-done((bf16[144,1536]{1,0:T(8,128)(2,1)S(1)}, bf16[144,1536]{1,0:T(8,128)(2,1)S(1)}, u32[]{:S(2)}, u32[]{:S(2)}) %collective-permute-start) | collective-permute-done | bytes 442400 | tf_op jit(solution)/shard_map/ppermute | solution.py:431
  41.9 8.3 %collective-permute-done.2.refs_3_.refs_7_ = bf16[144,1536]{1,0:T(8,128)(2,1)} collective-permute-done((bf16[144,1536]{1,0:T(8,128)(2,1)S(1)}, bf16[144,1536]{1,0:T(8,128)(2,1)}, u32[]{:S(2)}, u32[]{:S(2)}) %collective-permute-start.2) | collective-permute-done | bytes 442400 | tf_op jit(solution)/shard_map/ppermute | solution.py:431
  50.2 3.0 %norm.2 = (bf16[128,1536]{1,0:T(8,128)(2,1)S(1)}, bf16[128,1536]{1,0:T(8,128)(2,1)S(1)}, bf16[256,1536]{1,0:T(8,128)(2,1)S(1)}) custom-call(s32[2]{0:T(128)S(1)} %pad_add_fusion.key.at, bf16[144,1536]{1,0:T(8,128)(2,1)S(1)} %get-tuple-element.27.refs_0_.refs_4_, bf16[144,1536]{1,0:T(8,128)(2,1)S(1)} %collective-permute-done.refs_1_.refs_5_, ...), custom_call_target="tpu_custom_call" | custom-call | flops 100000000 | bytes 1000000 | tf_op jit(solution)/shard_map/norm/pallas_call | solution.py:340
  53.9 2.0 %collective-permute-start.7 = (bf16[128,1536]{1,0:T(8,128)(2,1)}, bf16[128,1536]{1,0:T(8,128)(2,1)S(1)}, u32[]{:S(2)}, u32[]{:S(2)}) collective-permute-start(bf16[128,1536]{1,0:T(8,128)(2,1)} %collective-permute-done.6.refs_2_), channel_id=1, source_target_pairs={{0,1},{1,0},{2,3},{3,2},{4,5},{5,4},{6,7},{7,6},{8,9},{9,8},{10,11... | collective-permute-start | bytes 1179656 | tf_op jit(solution)/shard_map/ppermute | solution.py:431
  57.3 8.8 %collective-permute-done.19.refs_1_ = bf16[128,1536]{1,0:T(8,128)(2,1)S(1)} collective-permute-done((bf16[128,1536]{1,0:T(8,128)(2,1)}, bf16[128,1536]{1,0:T(8,128)(2,1)S(1)}, u32[]{:S(2)}, u32[]{:S(2)}) %collective-permute-start.19) | collective-permute-done | bytes 393248 | tf_op jit(solution)/shard_map/ppermute | solution.py:431
  66.1 5.6 %collective-permute-done.7.refs_3_ = bf16[128,1536]{1,0:T(8,128)(2,1)S(1)} collective-permute-done((bf16[128,1536]{1,0:T(8,128)(2,1)}, bf16[128,1536]{1,0:T(8,128)(2,1)S(1)}, u32[]{:S(2)}, u32[]{:S(2)}) %collective-permute-start.7) | collective-permute-done | bytes 393248 | tf_op jit(solution)/shard_map/ppermute | solution.py:431
  71.7 2.9 %norm.3 = (bf16[128,1536]{1,0:T(8,128)(2,1)S(1)}, bf16[128,1536]{1,0:T(8,128)(2,1)S(1)}, bf16[256,1536]{1,0:T(8,128)(2,1)S(1)}) custom-call(s32[2]{0:T(128)S(1)} %pad_add_fusion.key.at, bf16[128,1536]{1,0:T(8,128)(2,1)} %second.1.refs_0_, bf16[128,1536]{1,0:T(8,128)(2,1)S(1)} %collective-permute-done.19.refs_1_, ...), custom_call_target="tpu_custom_call" | custom-call | flops 1000000000 | bytes 1000000 | tf_op jit(solution)/shard_map/norm/pallas_call | solution.py:340
  77.9 2.7 %project.4.kept = f32[2,128,2304]{2,1,0:T(8,128)S(1)} custom-call(bf16[128,1536]{1,0:T(8,128)(2,1)S(1)} %get-tuple-element.28.first, bf16[128,1536]{1,0:T(8,128)(2,1)S(1)} %get-tuple-element.56.second, bf16[3,1536,768]{2,1,0:T(8,128)(2,1)S(1)} %bitcast.44), custom_call_target="tpu_custom_call" | custom-call | flops 1000000000 | bytes 1000000 | tf_op jit(solution)/shard_map/project/pallas_call | solution.py:356
  80.6 10.8 %collective-permute-done.20 = bf16[256,1536]{1,0:T(8,128)(2,1)S(1)} collective-permute-done((bf16[256,1536]{1,0:T(8,128)(2,1)S(1)}, bf16[256,1536]{1,0:T(8,128)(2,1)S(1)}, u32[]{:S(2)}, u32[]{:S(2)}) %collective-permute-start.20) | collective-permute-done | bytes 786464 | tf_op jit(solution)/shard_map/ppermute | solution.py:425
  91.9 1.7 collective-permute-done.5.second
  94.7 2.6 %project.5 = f32[2,128,2304]{2,1,0:T(8,128)S(1)} custom-call(bf16[128,1536]{1,0:T(8,128)(2,1)S(1)} %collective-permute-done.4.first, bf16[128,1536]{1,0:T(8,128)(2,1)S(1)} %collective-permute-done.5.second, bf16[3,1536,768]{2,1,0:T(8,128)(2,1)S(1)} %bitcast.45), custom_call_target="tpu_custom_call" | custom-call | flops 1000000000 | bytes 1000000 | tf_op jit(solution)/shard_map/project/pallas_call | solution.py:356
  97.5 2.5 %project.7 = f32[2,128,2304]{2,1,0:T(8,128)S(1)} custom-call(bf16[128,1536]{1,0:T(8,128)(2,1)S(1)} %collective-permute-done.21.first, bf16[128,1536]{1,0:T(8,128)(2,1)S(1)} %collective-permute-done.22.second, bf16[3,1536,768]{2,1,0:T(8,128)(2,1)S(1)} %bitcast.46), custom_call_target="tpu_custom_call" | custom-call | flops 1000000000 | bytes 1000000 | tf_op jit(solution)/shard_map/project/pallas_call | solution.py:356
  100.9 2.5 %project.6.kept = f32[2,128,2304]{2,1,0:T(8,128)S(1)} custom-call(bf16[128,1536]{1,0:T(8,128)(2,1)S(1)} %get-tuple-element.37.first, bf16[128,1536]{1,0:T(8,128)(2,1)S(1)} %get-tuple-element.58.second, bf16[3,1536,768]{2,1,0:T(8,128)(2,1)S(1)} %bitcast.47), custom_call_target="tpu_custom_call" | custom-call | flops 99999997952 | bytes 1000000 | tf_op jit(solution)/shard_map/project/pallas_call | solution.py:356
  107.0 12.9 %collective-permute-done.11.over = bf16[128,2304]{1,0:T(8,128)(2,1)S(1)} collective-permute-done((bf16[128,2304]{1,0:T(8,128)(2,1)S(1)}, bf16[128,2304]{1,0:T(8,128)(2,1)S(1)}, u32[]{:S(2)}, u32[]{:S(2)}) %collective-permute-start.11) | collective-permute-done | bytes 589856 | tf_op jit(solution)/shard_map/ppermute | solution.py:425
  119.9 5.5 %attend.2 = (bf16[128,768]{1,0:T(8,128)(2,1)S(1)}, bf16[128,768]{1,0:T(8,128)(2,1)S(1)}, bf16[2,128,1536]{2,1,0:T(8,128)(2,1)S(1)}, bf16[128,1536]{1,0:T(8,128)(2,1)S(1)}, bf16[128,1536]{1,0:T(8,128)(2,1)S(1)}) custom-call(s32[2]{0:T(128)S(1)} %pad_add_fusion.key.at, f32[2,128,2304]{2,1,0:T(8,128)S(1)} %project.4.kept, ...), custom_call_target="tpu_custom_call" | custom-call | flops 1000000 | bytes 1000000 | tf_op jit(solution)/shard_map/attend/pallas_call | solution.py:382
  127.5 4.6 %collective-permute-done.24.over = bf16[128,2304]{1,0:T(8,128)(2,1)S(1)} collective-permute-done((bf16[128,2304]{1,0:T(8,128)(2,1)S(1)}, bf16[128,2304]{1,0:T(8,128)(2,1)S(1)}, u32[]{:S(2)}, u32[]{:S(2)}) %collective-permute-start.24) | collective-permute-done | bytes 589856 | tf_op jit(solution)/shard_map/ppermute | solution.py:425
  132.1 5.7 %attend.3 = (bf16[128,768]{1,0:T(8,128)(2,1)S(1)}, bf16[128,768]{1,0:T(8,128)(2,1)S(1)}, bf16[2,128,1536]{2,1,0:T(8,128)(2,1)S(1)}, bf16[128,1536]{1,0:T(8,128)(2,1)S(1)}, bf16[128,1536]{1,0:T(8,128)(2,1)S(1)}) custom-call(s32[2]{0:T(128)S(1)} %pad_add_fusion.key.at, f32[2,128,2304]{2,1,0:T(8,128)S(1)} %copy-done.1, ...), custom_call_target="tpu_custom_call" | custom-call | flops 1000000000 | bytes 1000000 | tf_op jit(solution)/shard_map/attend/pallas_call | solution.py:382
  138.6 3.4 %collective-permute-start.18 = (bf16[128,1536]{1,0:T(8,128)(2,1)S(1)}, bf16[128,1536]{1,0:T(8,128)(2,1)S(1)}, u32[]{:S(2)}, u32[]{:S(2)}) collective-permute-start(bf16[128,1536]{1,0:T(8,128)(2,1)S(1)} %fusion.7), channel_id=1, source_target_pairs={{0,2},{1,3},{2,0},{3,1},{4,6},{5,7},{6,4},{7,5},{8,10},{9,11},{10,... | collective-permute-start | bytes 1179656 | tf_op jit(solution)/shard_map/ppermute | solution.py:431
  142.0 19.1 %collective-permute-done.26 = bf16[128,1536]{1,0:T(8,128)(2,1)S(1)} collective-permute-done((bf16[128,1536]{1,0:T(8,128)(2,1)S(1)}, bf16[128,1536]{1,0:T(8,128)(2,1)S(1)}, u32[]{:S(2)}, u32[]{:S(2)}) %collective-permute-start.26) | collective-permute-done | bytes 393248 | tf_op jit(solution)/shard_map/ppermute | solution.py:431
  162.7 2.5 %collective-permute-start.25 = (bf16[128,1536]{1,0:T(8,128)(2,1)S(1)}, bf16[128,1536]{1,0:T(8,128)(2,1)S(1)}, u32[]{:S(2)}, u32[]{:S(2)}) collective-permute-start(bf16[128,1536]{1,0:T(8,128)(2,1)S(1)} %get-tuple-element.43), channel_id=1, source_target_pairs={{0,1},{1,0},{2,3},{3,2},{4,5},{5,4},{6,7},{7,6},{8,9},{9,8},{10,11... | collective-permute-start | bytes 1179656 | tf_op jit(solution)/shard_map/ppermute | solution.py:431
  166.8 13.3 %collective-permute-done.27 = bf16[128,1536]{1,0:T(8,128)(2,1)S(1)} collective-permute-done((bf16[128,1536]{1,0:T(8,128)(2,1)S(1)}, bf16[128,1536]{1,0:T(8,128)(2,1)S(1)}, u32[]{:S(2)}, u32[]{:S(2)}) %collective-permute-start.27) | collective-permute-done | bytes 393248 | tf_op jit(solution)/shard_map/ppermute | solution.py:431
  (97 shorter events, 29.9 us)
Async XLA Ops:
  4.3 23.9 %collective-permute-start.1 = (bf16[144,1536]{1,0:T(8,128)(2,1)S(1)}, bf16[144,1536]{1,0:T(8,128)(2,1)S(1)}, u32[]{:S(2)}, u32[]{:S(2)}) collective-permute-start(bf16[144,1536]{1,0:T(8,128)(2,1)S(1)} %get-tuple-element.27.refs_0_.refs_4_), channel_id=1, source_target_pairs={{0,2},{1,3},{2,0},{3,1},{4,6},{5,7},{6,4},{7,5},{8,10},{9,11},{10,... | collective-permute-start | bytes 1327112 | tf_op jit(solution)/shard_map/ppermute | solution.py:431
  11.2 46.0 %collective-permute-start.12 = (bf16[1280,768]{1,0:T(8,128)(2,1)}, bf16[1280,768]{1,0:T(8,128)(2,1)S(1)}, u32[]{:S(2)}, u32[]{:S(2)}) collective-permute-start(bf16[1280,768]{1,0:T(8,128)(2,1)} %pad_maximum_fusion), channel_id=1, source_target_pairs={{0,8},{4,12},{8,0},{12,4},{1,9},{5,13},{9,1},{13,5},{2,10},{6,14},... | collective-permute-start | bytes 5898248 | tf_op jit(solution)/shard_map/ppermute | solution.py:425
  12.7 29.2 %collective-permute-start = (bf16[144,1536]{1,0:T(8,128)(2,1)S(1)}, bf16[144,1536]{1,0:T(8,128)(2,1)S(1)}, u32[]{:S(2)}, u32[]{:S(2)}) collective-permute-start(bf16[144,1536]{1,0:T(8,128)(2,1)S(1)} %get-tuple-element.27.refs_0_.refs_4_), channel_id=1, source_target_pairs={{0,1},{1,0},{2,3},{3,2},{4,5},{5,4},{6,7},{7,6},{8,9},{9,8},{10,11... | collective-permute-start | bytes 1327112 | tf_op jit(solution)/shard_map/ppermute | solution.py:431
  14.3 79.5 %collective-permute-start.8 = (bf16[768,1536]{1,0:T(8,128)(2,1)}, bf16[768,1536]{1,0:T(8,128)(2,1)}, u32[]{:S(2)}, u32[]{:S(2)}) collective-permute-start(bf16[768,1536]{1,0:T(8,128)(2,1)} %o_own.3), channel_id=1, source_target_pairs={{0,4},{4,0},{8,12},{12,8},{1,5},{5,1},{9,13},{13,9},{2,6},{6,2},{1... | collective-permute-start | bytes 7077896 | tf_op jit(solution)/shard_map/ppermute | solution.py:425
  28.2 22.1 %collective-permute-start.2 = (bf16[144,1536]{1,0:T(8,128)(2,1)S(1)}, bf16[144,1536]{1,0:T(8,128)(2,1)}, u32[]{:S(2)}, u32[]{:S(2)}) collective-permute-start(bf16[144,1536]{1,0:T(8,128)(2,1)S(1)} %collective-permute-done.1.refs_2_.refs_6_), channel_id=1, source_target_pairs={{0,1},{1,0},{2,3},{3,2},{4,5},{5,4},{6,7},{7,6},{8,9},{9,8},{10,11... | collective-permute-start | bytes 1327112 | tf_op jit(solution)/shard_map/ppermute | solution.py:431
  29.6 24.2 %collective-permute-start.6 = (bf16[128,1536]{1,0:T(8,128)(2,1)}, bf16[128,1536]{1,0:T(8,128)(2,1)}, u32[]{:S(2)}, u32[]{:S(2)}) collective-permute-start(bf16[128,1536]{1,0:T(8,128)(2,1)} %second.1.refs_0_), channel_id=1, source_target_pairs={{0,2},{1,3},{2,0},{3,1},{4,6},{5,7},{6,4},{7,5},{8,10},{9,11},{10,... | collective-permute-start | bytes 1179656 | tf_op jit(solution)/shard_map/ppermute | solution.py:431
  53.2 22.9 %collective-permute-start.3 = (bf16[256,1536]{1,0:T(8,128)(2,1)S(1)}, bf16[256,1536]{1,0:T(8,128)(2,1)S(1)}, u32[]{:S(2)}, u32[]{:S(2)}) collective-permute-start(bf16[256,1536]{1,0:T(8,128)(2,1)S(1)} %get-tuple-element.29), channel_id=1, source_target_pairs={{0,8},{4,12},{8,0},{12,4},{1,9},{5,13},{9,1},{13,5},{2,10},{6,14},... | collective-permute-start | bytes 2359304 | tf_op jit(solution)/shard_map/ppermute | solution.py:425
  53.8 12.3 %collective-permute-start.19 = (bf16[128,1536]{1,0:T(8,128)(2,1)}, bf16[128,1536]{1,0:T(8,128)(2,1)S(1)}, u32[]{:S(2)}, u32[]{:S(2)}) collective-permute-start(bf16[128,1536]{1,0:T(8,128)(2,1)} %second.1.refs_0_), channel_id=1, source_target_pairs={{0,1},{1,0},{2,3},{3,2},{4,5},{5,4},{6,7},{7,6},{8,9},{9,8},{10,11... | collective-permute-start | bytes 1179656 | tf_op jit(solution)/shard_map/ppermute | solution.py:431
  53.9 17.8 %collective-permute-start.7 = (bf16[128,1536]{1,0:T(8,128)(2,1)}, bf16[128,1536]{1,0:T(8,128)(2,1)S(1)}, u32[]{:S(2)}, u32[]{:S(2)}) collective-permute-start(bf16[128,1536]{1,0:T(8,128)(2,1)} %collective-permute-done.6.refs_2_), channel_id=1, source_target_pairs={{0,1},{1,0},{2,3},{3,2},{4,5},{5,4},{6,7},{7,6},{8,9},{9,8},{10,11... | collective-permute-start | bytes 1179656 | tf_op jit(solution)/shard_map/ppermute | solution.py:431
  57.2 43.8 %collective-permute-start.13 = (bf16[1280,768]{1,0:T(8,128)(2,1)S(1)}, bf16[1280,768]{1,0:T(8,128)(2,1)S(1)}, u32[]{:S(2)}, u32[]{:S(2)}) collective-permute-start(bf16[1280,768]{1,0:T(8,128)(2,1)S(1)} %collective-permute-done.12.k_x.v_x.o_x), channel_id=1, source_target_pairs={{0,4},{4,0},{8,12},{12,8},{1,5},{5,1},{9,13},{13,9},{2,6},{6,2},{1... | collective-permute-start | bytes 5898248 | tf_op jit(solution)/shard_map/ppermute | solution.py:425
  66.1 25.3 %collective-permute-start.9 = (bf16[512,768]{1,0:T(8,128)(2,1)S(1)}, bf16[512,768]{1,0:T(8,128)(2,1)S(1)}, u32[]{:S(2)}, u32[]{:S(2)}) collective-permute-start(bf16[512,768]{1,0:T(8,128)(2,1)S(1)} %pad_maximum_fusion.1), channel_id=1, source_target_pairs={{0,4},{4,0},{8,12},{12,8},{1,5},{5,1},{9,13},{13,9},{2,6},{6,2},{1... | collective-permute-start | bytes 2359304 | tf_op jit(solution)/shard_map/ppermute | solution.py:425
  74.6 16.8 %collective-permute-start.20 = (bf16[256,1536]{1,0:T(8,128)(2,1)S(1)}, bf16[256,1536]{1,0:T(8,128)(2,1)S(1)}, u32[]{:S(2)}, u32[]{:S(2)}) collective-permute-start(bf16[256,1536]{1,0:T(8,128)(2,1)S(1)} %get-tuple-element.38), channel_id=1, source_target_pairs={{0,8},{4,12},{8,0},{12,4},{1,9},{5,13},{9,1},{13,5},{2,10},{6,14},... | collective-permute-start | bytes 2359304 | tf_op jit(solution)/shard_map/ppermute | solution.py:425
  76.1 24.8 %collective-permute-start.14 = (bf16[768,768]{1,0:T(8,128)(2,1)S(1)}, bf16[768,768]{1,0:T(8,128)(2,1)S(1)}, u32[]{:S(2)}, u32[]{:S(2)}) collective-permute-start(bf16[768,768]{1,0:T(8,128)(2,1)S(1)} %slice.80), channel_id=1, source_target_pairs={{0,16},{16,0},{1,17},{17,1},{2,18},{18,2},{3,19},{19,3},{4,20},{20... | collective-permute-start | bytes 3538952 | tf_op jit(solution)/shard_map/ppermute | solution.py:428
  97.3 6.2 %collective-permute-start.10 = (f32[2,128,2304]{2,1,0:T(8,128)S(1)}, f32[2,128,2304]{2,1,0:T(8,128)S(1)}, u32[]{:S(2)}, u32[]{:S(2)}) collective-permute-start(f32[2,128,2304]{2,1,0:T(8,128)S(1)} %project.5), channel_id=1, source_target_pairs={{0,4},{4,0},{8,12},{12,8},{1,5},{5,1},{9,13},{13,9},{2,6},{6,2},{1... | collective-permute-start | bytes 7077896 | tf_op jit(solution)/shard_map/ppermute | solution.py:425
  100.0 5.2 %collective-permute-start.23 = (f32[2,128,2304]{2,1,0:T(8,128)S(1)}, f32[2,128,2304]{2,1,0:T(8,128)S(1)}, u32[]{:S(2)}, u32[]{:S(2)}) collective-permute-start(f32[2,128,2304]{2,1,0:T(8,128)S(1)} %project.7), channel_id=1, source_target_pairs={{0,4},{4,0},{8,12},{12,8},{1,5},{5,1},{9,13},{13,9},{2,6},{6,2},{1... | collective-permute-start | bytes 7077896 | tf_op jit(solution)/shard_map/ppermute | solution.py:425
  100.9 6.0 %collective-permute-start.15 = (bf16[768,768]{1,0:T(8,128)(2,1)S(1)}, bf16[768,768]{1,0:T(8,128)(2,1)S(1)}, u32[]{:S(2)}, u32[]{:S(2)}) collective-permute-start(bf16[768,768]{1,0:T(8,128)(2,1)S(1)} %collective-permute-done.14.o_y), channel_id=1, source_target_pairs={{0,4},{4,0},{8,12},{12,8},{1,5},{5,1},{9,13},{13,9},{2,6},{6,2},{1... | collective-permute-start | bytes 3538952 | tf_op jit(solution)/shard_map/ppermute | solution.py:425
  103.7 16.2 %collective-permute-start.11 = (bf16[128,2304]{1,0:T(8,128)(2,1)S(1)}, bf16[128,2304]{1,0:T(8,128)(2,1)S(1)}, u32[]{:S(2)}, u32[]{:S(2)}) collective-permute-start(bf16[128,2304]{1,0:T(8,128)(2,1)S(1)} %fusion.12), channel_id=1, source_target_pairs={{0,8},{4,12},{8,0},{12,4},{1,9},{5,13},{9,1},{13,5},{2,10},{6,14},... | collective-permute-start | bytes 1769480 | tf_op jit(solution)/shard_map/ppermute | solution.py:425
  105.4 26.7 %collective-permute-start.24 = (bf16[128,2304]{1,0:T(8,128)(2,1)S(1)}, bf16[128,2304]{1,0:T(8,128)(2,1)S(1)}, u32[]{:S(2)}, u32[]{:S(2)}) collective-permute-start(bf16[128,2304]{1,0:T(8,128)(2,1)S(1)} %fusion.13), channel_id=1, source_target_pairs={{0,8},{4,12},{8,0},{12,4},{1,9},{5,13},{9,1},{13,5},{2,10},{6,14},... | collective-permute-start | bytes 1769480 | tf_op jit(solution)/shard_map/ppermute | solution.py:425
  125.4 13.1 %collective-permute-start.17 = (bf16[128,1536]{1,0:T(8,128)(2,1)S(1)}, bf16[128,1536]{1,0:T(8,128)(2,1)S(1)}, u32[]{:S(2)}, u32[]{:S(2)}) collective-permute-start(bf16[128,1536]{1,0:T(8,128)(2,1)S(1)} %get-tuple-element.35), channel_id=1, source_target_pairs={{0,1},{1,0},{2,3},{3,2},{4,5},{5,4},{6,7},{7,6},{8,9},{9,8},{10,11... | collective-permute-start | bytes 1179656 | tf_op jit(solution)/shard_map/ppermute | solution.py:431
  126.0 40.8 %collective-permute-start.16 = (bf16[128,1536]{1,0:T(8,128)(2,1)S(1)}, bf16[128,1536]{1,0:T(8,128)(2,1)S(1)}, u32[]{:S(2)}, u32[]{:S(2)}) collective-permute-start(bf16[128,1536]{1,0:T(8,128)(2,1)S(1)} %get-tuple-element.34), channel_id=1, source_target_pairs={{0,1},{1,0},{2,3},{3,2},{4,5},{5,4},{6,7},{7,6},{8,9},{9,8},{10,11... | collective-permute-start | bytes 1179656 | tf_op jit(solution)/shard_map/ppermute | solution.py:431
  137.9 23.2 %collective-permute-start.26 = (bf16[128,1536]{1,0:T(8,128)(2,1)S(1)}, bf16[128,1536]{1,0:T(8,128)(2,1)S(1)}, u32[]{:S(2)}, u32[]{:S(2)}) collective-permute-start(bf16[128,1536]{1,0:T(8,128)(2,1)S(1)} %get-tuple-element.44), channel_id=1, source_target_pairs={{0,1},{1,0},{2,3},{3,2},{4,5},{5,4},{6,7},{7,6},{8,9},{9,8},{10,11... | collective-permute-start | bytes 1179656 | tf_op jit(solution)/shard_map/ppermute | solution.py:431
  138.6 24.1 %collective-permute-start.18 = (bf16[128,1536]{1,0:T(8,128)(2,1)S(1)}, bf16[128,1536]{1,0:T(8,128)(2,1)S(1)}, u32[]{:S(2)}, u32[]{:S(2)}) collective-permute-start(bf16[128,1536]{1,0:T(8,128)(2,1)S(1)} %fusion.7), channel_id=1, source_target_pairs={{0,2},{1,3},{2,0},{3,1},{4,6},{5,7},{6,4},{7,5},{8,10},{9,11},{10,... | collective-permute-start | bytes 1179656 | tf_op jit(solution)/shard_map/ppermute | solution.py:431
  161.2 18.9 %collective-permute-start.27 = (bf16[128,1536]{1,0:T(8,128)(2,1)S(1)}, bf16[128,1536]{1,0:T(8,128)(2,1)S(1)}, u32[]{:S(2)}, u32[]{:S(2)}) collective-permute-start(bf16[128,1536]{1,0:T(8,128)(2,1)S(1)} %fusion.2), channel_id=1, source_target_pairs={{0,2},{1,3},{2,0},{3,1},{4,6},{5,7},{6,4},{7,5},{8,10},{9,11},{10,... | collective-permute-start | bytes 1179656 | tf_op jit(solution)/shard_map/ppermute | solution.py:431
  162.7 17.5 %collective-permute-start.25 = (bf16[128,1536]{1,0:T(8,128)(2,1)S(1)}, bf16[128,1536]{1,0:T(8,128)(2,1)S(1)}, u32[]{:S(2)}, u32[]{:S(2)}) collective-permute-start(bf16[128,1536]{1,0:T(8,128)(2,1)S(1)} %get-tuple-element.43), channel_id=1, source_target_pairs={{0,1},{1,0},{2,3},{3,2},{4,5},{5,4},{6,7},{7,6},{8,9},{9,8},{10,11... | collective-permute-start | bytes 1179656 | tf_op jit(solution)/shard_map/ppermute | solution.py:431
  (20 other events, 242.9 us)

commit v4 on v3

--- a/solution.py
+++ b/solution.py
@@ -199,6 +199,10 @@
     product = jnp.dot(held[...], weight[0], preferred_element_type=jnp.float32)
     out[0] = product[:rows]
     out[1] = product[rows:]
+
+
+def merge_kernel(kept, back, out):
+    out[...] = (kept[0] + back[0]).astype(jnp.bfloat16)
 
 
 def attend_kernel(
@@ -273,26 +277,33 @@
     far_three[...] = held[3]
 
 
-TIES = {'kept1': ('cross_far',),
- 'last1': ('rest0',),
- 'late': ('two0',),
- 'sent0': ('three1', 'o_pair', 's_pair'),
+TIES = {'away0': ('far',),
+ 'cross_y': ('back0',),
+ 'kept0': ('o_pair',),
+ 'kept1': ('back0', 'back1', 'cross_far'),
+ 'last1': ('come1',),
+ 'norm1': ('far',),
+ 'one1': ('two1',),
+ 'pair1': ('away0',),
+ 's_pair': ('far',),
+ 'sent0': ('mine1', 'o_pair', 'one1', 's_pair'),
  'sent0_last': (),
- 'sent1_last': (),
- 'use1': ('kept0',)}
+ 'turned1': ('o_y',)}
 WORK = {'attend0': 6,
  'attend1': 9,
- 'kept0': 9,
- 'kept1': 11,
- 'norm0': 8,
- 'norm1': 9,
- 'second': 10,
+ 'kept0': 10.5,
+ 'kept1': 10,
+ 'merge0': 10.6,
+ 'merge1': 9,
+ 'norm0': 10,
+ 'norm1': 11,
+ 'second': 6,
  'sent0': 9,
  'sent1': 9}
 
 
 def cost(name):
-    return pl.CostEstimate(flops=10 ** WORK[name], bytes_accessed=10**6, transcendentals=0)
+    return pl.CostEstimate(flops=int(10 ** WORK[name]), bytes_accessed=10**6, transcendentals=0)
 
 
 def params(mebibytes):
@@ -364,6 +375,21 @@
         cost_estimate=cost(name),
         name="project",
     )(first, second, weight)
+
+
+def run_merge(name, kept, back):
+    _, rows, cols = kept.shape
+    half = pl.BlockSpec((1, rows, cols), lambda i: (1, 0, 0))
+    return pl.pallas_call(
+        merge_kernel,
+        grid=(1,),
+        in_specs=[half, half],
+        out_specs=pl.BlockSpec((rows, cols), lambda i: (0, 0)),
+        out_shape=jax.ShapeDtypeStruct((rows, cols), jnp.bfloat16),
+        compiler_params=params(16),
+        cost_estimate=cost(name),
+        name="merge",
+    )(kept, back)
 
 
 def run_attend(s, at, kept, back, over, stale, tables, gains, columns):
@@ -494,17 +520,16 @@
     for s in range(samples):
         mine, pair, away = shared[s]
         away = tie(f"use{s}", away)
-        over, cross = away[:rows], make(f"cross{s}", to_f(away[rows:], 1))
+        over, cross = away[:rows], make(f"cross{s}", to_f(tie(f"cross{s}", away[rows:]), 1))
         if s == 1:
             cross_y = make("cross_y", to_f(tie("cross_y", o_y), 1))
         if f"sent{s}_last" in TIES:
             kept = make(f"kept{s}", run_project(f"kept{s}", tie(f"kept{s}", mine), over, weight))
-            sent = run_project(f"sent{s}", pair, tie(f"sent{s}", cross), weight)
-        else:
-            sent = run_project(f"sent{s}", pair, tie(f"sent{s}", cross), weight)
+        sent = make(f"sent{s}", run_project(f"sent{s}", pair, tie(f"sent{s}", cross), weight))
+        back = make(f"back{s}", to_f(tie(f"back{s}", sent), 1))
+        if f"sent{s}_last" not in TIES:
             kept = make(f"kept{s}", run_project(f"kept{s}", tie(f"kept{s}", mine), over, weight))
-        back = make(f"back{s}", to_f(sent, 1))
-        part = make(f"part{s}", (kept[1] + back[1]).astype(jnp.bfloat16))
+        part = make(f"part{s}", run_merge(f"merge{s}", kept, back))
         halves.append((kept, back))
         turned.append(make(f"turned{s}", to_f(tie(f"turned{s}", part), 2)))
     columns = (out_weight, o_pair, far, o_y, cross_far, cross_y)

time: 182 us -> 178 us (0.978)
  local copies, waits for them, and re-layouts: 4.42 us -> 1.68 us
    ppermute x15, waiting for transfers between devices: 31.9 us -> 28.5 us  [to_f(): return lax.ppermute(v, 'fsdp', [(i, i ^ d) for i in range(4)])]
    unnamed x32 -> x26, local copies, waits for them, and re-layouts: 2.89 us -> 0.07 us
  transfers between devices with their start and end apart: 28 -> 28, of which waited for: 15 -> 13; matrix products, arithmetic and copies ran while one was open for 3% -> 2% of each run, Pallas kernels for 16% -> 16%
where the time goes in v4:
time: 178 us
  waiting for transfers between devices  109 us (61%)
  starting transfers between devices  31 us (17%)
  Pallas kernels  28.4 us (16%)
  other arithmetic  6.58 us (4%)
    ppermute x12, waiting for transfers between devices, to_z(): return lax.ppermute(v, 'patch', [(i, i ^ d) for i in range(4)])  78.3 us
    ppermute x15, waiting for transfers between devices, to_f(): return lax.ppermute(v, 'fsdp', [(i, i ^ d) for i in range(4)])  28.5 us
    ppermute x12, starting transfers between devices, to_z(): return lax.ppermute(v, 'patch', [(i, i ^ d) for i in range(4)])  22.1 us
    pallas_call x2, Pallas kernels, run_attend(): pl.pallas_call(attend_kernel, grid_spec=pltpu.PrefetchScalarGridSpec(num_...  11.1 us
    pallas_call x4, Pallas kernels, run_project(): pl.pallas_call(project_kernel, grid=(3,), in_specs=[vmem] * 2 + [pl.Block...  10.3 us
    ppermute x15, starting transfers between devices, to_f(): return lax.ppermute(v, 'fsdp', [(i, i ^ d) for i in range(4)])  7.28 us
    pallas_call x2, Pallas kernels, run_norm(): pl.pallas_call(functools.partial(norm_kernel, s), in_specs=[pl.BlockSpec(...  5.88 us
  transfers between devices with their start and end apart: 28, of which 13 were waited for; matrix products, arithmetic and copies ran while one was open for 2% of the time, Pallas kernels for 16%

profile of v4, /device:TPU:0, one launch (start us, length us, event | category | flops | bytes accessed | tf_op | source)
XLA Modules:
  0.0 177.6 jit_solution(1730754028054671756)
XLA Ops:
  3.6 2.9 %collective-permute-start.4 = (bf16[1280,768]{1,0:T(8,128)(2,1)}, bf16[1280,768]{1,0:T(8,128)(2,1)S(1)}, u32[]{:S(2)}, u32[]{:S(2)}) collective-permute-start(bf16[1280,768]{1,0:T(8,128)(2,1)} %pad_maximum_fusion), channel_id=1, source_target_pairs={{0,8},{4,12},{8,0},{12,4},{1,9},{5,13},{9,1},{13,5},{2,10},{6,14},... | collective-permute-start | bytes 5898248 | tf_op jit(solution)/shard_map/ppermute | solution.py:451
  7.4 2.7 %collective-permute-start.1 = (bf16[144,1536]{1,0:T(8,128)(2,1)S(1)}, bf16[144,1536]{1,0:T(8,128)(2,1)}, u32[]{:S(2)}, u32[]{:S(2)}) collective-permute-start(bf16[144,1536]{1,0:T(8,128)(2,1)S(1)} %get-tuple-element.33.refs_0_.refs_4_), channel_id=1, source_target_pairs={{0,2},{1,3},{2,0},{3,1},{4,6},{5,7},{6,4},{7,5},{8,10},{9,11},{10,... | collective-permute-start | bytes 1327112 | tf_op jit(solution)/shard_map/ppermute | solution.py:457
  12.0 25.8 %collective-permute-done.1.refs_2_.refs_6_ = bf16[144,1536]{1,0:T(8,128)(2,1)} collective-permute-done((bf16[144,1536]{1,0:T(8,128)(2,1)S(1)}, bf16[144,1536]{1,0:T(8,128)(2,1)}, u32[]{:S(2)}, u32[]{:S(2)}) %collective-permute-start.1) | collective-permute-done | bytes 442400 | tf_op jit(solution)/shard_map/ppermute | solution.py:457
  39.1 7.3 %collective-permute-done.8.refs_2_ = bf16[128,1536]{1,0:T(8,128)(2,1)S(1)} collective-permute-done((bf16[128,1536]{1,0:T(8,128)(2,1)S(1)}, bf16[128,1536]{1,0:T(8,128)(2,1)S(1)}, u32[]{:S(2)}, u32[]{:S(2)}) %collective-permute-start.8) | collective-permute-done | bytes 393248 | tf_op jit(solution)/shard_map/ppermute | solution.py:457
  48.5 5.7 %collective-permute-done.2.refs_3_.refs_7_ = bf16[144,1536]{1,0:T(8,128)(2,1)S(1)} collective-permute-done((bf16[144,1536]{1,0:T(8,128)(2,1)}, bf16[144,1536]{1,0:T(8,128)(2,1)S(1)}, u32[]{:S(2)}, u32[]{:S(2)}) %collective-permute-start.2) | collective-permute-done | bytes 442400 | tf_op jit(solution)/shard_map/ppermute | solution.py:457
  54.2 3.1 %norm.2 = (bf16[128,1536]{1,0:T(8,128)(2,1)S(1)}, bf16[128,1536]{1,0:T(8,128)(2,1)S(1)}, bf16[256,1536]{1,0:T(8,128)(2,1)S(1)}) custom-call(s32[2]{0:T(128)S(1)} %pad_add_fusion.key.at, bf16[144,1536]{1,0:T(8,128)(2,1)S(1)} %get-tuple-element.33.refs_0_.refs_4_, bf16[144,1536]{1,0:T(8,128)(2,1)} %collective-permute-done.refs_1_.refs_5_, ...), custom_call_target="tpu_custom_call" | custom-call | flops 10000000000 | bytes 1000000 | tf_op jit(solution)/shard_map/norm/pallas_call | solution.py:351
  57.8 10.1 %collective-permute-done.10.refs_3_ = bf16[128,1536]{1,0:T(8,128)(2,1)S(1)} collective-permute-done((bf16[128,1536]{1,0:T(8,128)(2,1)S(1)}, bf16[128,1536]{1,0:T(8,128)(2,1)S(1)}, u32[]{:S(2)}, u32[]{:S(2)}) %collective-permute-start.10) | collective-permute-done | bytes 393248 | tf_op jit(solution)/shard_map/ppermute | solution.py:457
  67.9 2.8 %norm.3 = (bf16[128,1536]{1,0:T(8,128)(2,1)S(1)}, bf16[128,1536]{1,0:T(8,128)(2,1)S(1)}, bf16[256,1536]{1,0:T(8,128)(2,1)S(1)}) custom-call(s32[2]{0:T(128)S(1)} %pad_add_fusion.key.at, bf16[128,1536]{1,0:T(8,128)(2,1)S(1)} %second.1.refs_0_, bf16[128,1536]{1,0:T(8,128)(2,1)S(1)} %collective-permute-done.9.refs_1_, ...), custom_call_target="tpu_custom_call" | custom-call | flops 99999997952 | bytes 1000000 | tf_op jit(solution)/shard_map/norm/pallas_call | solution.py:351
  72.5 1.6 collective-permute-start.15
  74.2 13.1 %collective-permute-done.21 = bf16[256,1536]{1,0:T(8,128)(2,1)S(1)} collective-permute-done((bf16[256,1536]{1,0:T(8,128)(2,1)S(1)}, bf16[256,1536]{1,0:T(8,128)(2,1)S(1)}, u32[]{:S(2)}, u32[]{:S(2)}) %collective-permute-start.21) | collective-permute-done | bytes 786464 | tf_op jit(solution)/shard_map/ppermute | solution.py:451
  89.1 2.7 %project.5 = f32[2,128,2304]{2,1,0:T(8,128)S(1)} custom-call(bf16[128,1536]{1,0:T(8,128)(2,1)S(1)} %collective-permute-done.6.first, bf16[128,1536]{1,0:T(8,128)(2,1)S(1)} %collective-permute-done.7.second, bf16[3,1536,768]{2,1,0:T(8,128)(2,1)S(1)} %bitcast.40), custom_call_target="tpu_custom_call" | custom-call | flops 1000000000 | bytes 1000000 | tf_op jit(solution)/shard_map/project/pallas_call | solution.py:367
  92.3 2.5 %project.4.kept = f32[2,128,2304]{2,1,0:T(8,128)S(1)} custom-call(bf16[128,1536]{1,0:T(8,128)(2,1)S(1)} %get-tuple-element.35.first, bf16[128,1536]{1,0:T(8,128)(2,1)S(1)} %get-tuple-element.67.second, bf16[3,1536,768]{2,1,0:T(8,128)(2,1)S(1)} %bitcast.41), custom_call_target="tpu_custom_call" | custom-call | flops 31622776832 | bytes 1000000 | tf_op jit(solution)/shard_map/project/pallas_call | solution.py:367
  94.9 2.5 %project.6 = f32[2,128,2304]{2,1,0:T(8,128)S(1)} custom-call(bf16[128,1536]{1,0:T(8,128)(2,1)S(1)} %collective-permute-done.20.first, bf16[128,1536]{1,0:T(8,128)(2,1)S(1)} %collective-permute-done.22.second, bf16[3,1536,768]{2,1,0:T(8,128)(2,1)S(1)} %bitcast.42), custom_call_target="tpu_custom_call" | custom-call | flops 1000000000 | bytes 1000000 | tf_op jit(solution)/shard_map/project/pallas_call | solution.py:367
  98.4 2.2 %collective-permute-done.15.o_y = bf16[768,768]{1,0:T(8,128)(2,1)S(1)} collective-permute-done((bf16[768,768]{1,0:T(8,128)(2,1)S(1)}, bf16[768,768]{1,0:T(8,128)(2,1)S(1)}, u32[]{:S(2)}, u32[]{:S(2)}) %collective-permute-start.15) | collective-permute-done | bytes 1179680 | tf_op jit(solution)/shard_map/ppermute | solution.py:454
  102.0 2.5 %project.7.kept = f32[2,128,2304]{2,1,0:T(8,128)S(1)} custom-call(bf16[128,1536]{1,0:T(8,128)(2,1)S(1)} %get-tuple-element.51.first, bf16[128,1536]{1,0:T(8,128)(2,1)S(1)} %get-tuple-element.69.second, bf16[3,1536,768]{2,1,0:T(8,128)(2,1)S(1)} %bitcast.43), custom_call_target="tpu_custom_call" | custom-call | flops 10000000000 | bytes 1000000 | tf_op jit(solution)/shard_map/project/pallas_call | solution.py:367
  105.6 8.4 %collective-permute-done.13.over = bf16[128,2304]{1,0:T(8,128)(2,1)S(1)} collective-permute-done((bf16[128,2304]{1,0:T(8,128)(2,1)S(1)}, bf16[128,2304]{1,0:T(8,128)(2,1)S(1)}, u32[]{:S(2)}, u32[]{:S(2)}) %collective-permute-start.13) | collective-permute-done | bytes 589856 | tf_op jit(solution)/shard_map/ppermute | solution.py:451
  114.0 5.5 %attend.2 = (bf16[128,768]{1,0:T(8,128)(2,1)S(1)}, bf16[128,768]{1,0:T(8,128)(2,1)S(1)}, bf16[2,128,1536]{2,1,0:T(8,128)(2,1)S(1)}, bf16[128,1536]{1,0:T(8,128)(2,1)S(1)}, bf16[128,1536]{1,0:T(8,128)(2,1)S(1)}) custom-call(s32[2]{0:T(128)S(1)} %pad_add_fusion.key.at, f32[2,128,2304]{2,1,0:T(8,128)S(1)} %copy-done.3, ...), custom_call_target="tpu_custom_call" | custom-call | flops 1000000 | bytes 1000000 | tf_op jit(solution)/shard_map/attend/pallas_call | solution.py:408
  121.6 4.4 %collective-permute-done.24.over = bf16[128,2304]{1,0:T(8,128)(2,1)S(1)} collective-permute-done((bf16[128,2304]{1,0:T(8,128)(2,1)S(1)}, bf16[128,2304]{1,0:T(8,128)(2,1)S(1)}, u32[]{:S(2)}, u32[]{:S(2)}) %collective-permute-start.24) | collective-permute-done | bytes 589856 | tf_op jit(solution)/shard_map/ppermute | solution.py:451
  126.1 5.5 %attend.3 = (bf16[128,768]{1,0:T(8,128)(2,1)S(1)}, bf16[128,768]{1,0:T(8,128)(2,1)S(1)}, bf16[2,128,1536]{2,1,0:T(8,128)(2,1)S(1)}, bf16[128,1536]{1,0:T(8,128)(2,1)S(1)}, bf16[128,1536]{1,0:T(8,128)(2,1)S(1)}) custom-call(s32[2]{0:T(128)S(1)} %pad_add_fusion.key.at, f32[2,128,2304]{2,1,0:T(8,128)S(1)} %project.7.kept, ...), custom_call_target="tpu_custom_call" | custom-call | flops 1000000000 | bytes 1000000 | tf_op jit(solution)/shard_map/attend/pallas_call | solution.py:408
  132.5 6.0 %collective-permute-start.19 = (bf16[128,1536]{1,0:T(8,128)(2,1)S(1)}, bf16[128,1536]{1,0:T(8,128)(2,1)S(1)}, u32[]{:S(2)}, u32[]{:S(2)}) collective-permute-start(bf16[128,1536]{1,0:T(8,128)(2,1)S(1)} %fusion.5), channel_id=1, source_target_pairs={{0,2},{1,3},{2,0},{3,1},{4,6},{5,7},{6,4},{7,5},{8,10},{9,11},{10,... | collective-permute-start | bytes 1179656 | tf_op jit(solution)/shard_map/ppermute | solution.py:457
  138.5 16.5 %collective-permute-done.25 = bf16[128,1536]{1,0:T(8,128)(2,1)S(1)} collective-permute-done((bf16[128,1536]{1,0:T(8,128)(2,1)S(1)}, bf16[128,1536]{1,0:T(8,128)(2,1)S(1)}, u32[]{:S(2)}, u32[]{:S(2)}) %collective-permute-start.25) | collective-permute-done | bytes 393248 | tf_op jit(solution)/shard_map/ppermute | solution.py:457
  155.0 4.2 %collective-permute-start.27 = (bf16[128,1536]{1,0:T(8,128)(2,1)S(1)}, bf16[128,1536]{1,0:T(8,128)(2,1)S(1)}, u32[]{:S(2)}, u32[]{:S(2)}) collective-permute-start(bf16[128,1536]{1,0:T(8,128)(2,1)S(1)} %fusion), channel_id=1, source_target_pairs={{0,2},{1,3},{2,0},{3,1},{4,6},{5,7},{6,4},{7,5},{8,10},{9,11},{10,... | collective-permute-start | bytes 1179656 | tf_op jit(solution)/shard_map/ppermute | solution.py:457
  159.2 2.5 %collective-permute-start.26 = (bf16[128,1536]{1,0:T(8,128)(2,1)S(1)}, bf16[128,1536]{1,0:T(8,128)(2,1)S(1)}, u32[]{:S(2)}, u32[]{:S(2)}) collective-permute-start(bf16[128,1536]{1,0:T(8,128)(2,1)S(1)} %get-tuple-element.56), channel_id=1, source_target_pairs={{0,1},{1,0},{2,3},{3,2},{4,5},{5,4},{6,7},{7,6},{8,9},{9,8},{10,11... | collective-permute-start | bytes 1179656 | tf_op jit(solution)/shard_map/ppermute | solution.py:457
  163.3 12.9 %collective-permute-done.27 = bf16[128,1536]{1,0:T(8,128)(2,1)S(1)} collective-permute-done((bf16[128,1536]{1,0:T(8,128)(2,1)S(1)}, bf16[128,1536]{1,0:T(8,128)(2,1)S(1)}, u32[]{:S(2)}, u32[]{:S(2)}) %collective-permute-start.27) | collective-permute-done | bytes 393248 | tf_op jit(solution)/shard_map/ppermute | solution.py:457
  (91 shorter events, 23.2 us)
Async XLA Ops:
  3.6 53.7 %collective-permute-start.4 = (bf16[1280,768]{1,0:T(8,128)(2,1)}, bf16[1280,768]{1,0:T(8,128)(2,1)S(1)}, u32[]{:S(2)}, u32[]{:S(2)}) collective-permute-start(bf16[1280,768]{1,0:T(8,128)(2,1)} %pad_maximum_fusion), channel_id=1, source_target_pairs={{0,8},{4,12},{8,0},{12,4},{1,9},{5,13},{9,1},{13,5},{2,10},{6,14},... | collective-permute-start | bytes 5898248 | tf_op jit(solution)/shard_map/ppermute | solution.py:451
  7.4 30.5 %collective-permute-start.1 = (bf16[144,1536]{1,0:T(8,128)(2,1)S(1)}, bf16[144,1536]{1,0:T(8,128)(2,1)}, u32[]{:S(2)}, u32[]{:S(2)}) collective-permute-start(bf16[144,1536]{1,0:T(8,128)(2,1)S(1)} %get-tuple-element.33.refs_0_.refs_4_), channel_id=1, source_target_pairs={{0,2},{1,3},{2,0},{3,1},{4,6},{5,7},{6,4},{7,5},{8,10},{9,11},{10,... | collective-permute-start | bytes 1327112 | tf_op jit(solution)/shard_map/ppermute | solution.py:457
  10.0 37.0 %collective-permute-start = (bf16[144,1536]{1,0:T(8,128)(2,1)S(1)}, bf16[144,1536]{1,0:T(8,128)(2,1)}, u32[]{:S(2)}, u32[]{:S(2)}) collective-permute-start(bf16[144,1536]{1,0:T(8,128)(2,1)S(1)} %get-tuple-element.33.refs_0_.refs_4_), channel_id=1, source_target_pairs={{0,1},{1,0},{2,3},{3,2},{4,5},{5,4},{6,7},{7,6},{8,9},{9,8},{10,11... | collective-permute-start | bytes 1327112 | tf_op jit(solution)/shard_map/ppermute | solution.py:457
  11.6 61.0 %collective-permute-start.3 = (bf16[768,1536]{1,0:T(8,128)(2,1)}, bf16[768,1536]{1,0:T(8,128)(2,1)}, u32[]{:S(2)}, u32[]{:S(2)}) collective-permute-start(bf16[768,1536]{1,0:T(8,128)(2,1)} %o_own.3), channel_id=1, source_target_pairs={{0,4},{4,0},{8,12},{12,8},{1,5},{5,1},{9,13},{13,9},{2,6},{6,2},{1... | collective-permute-start | bytes 7077896 | tf_op jit(solution)/shard_map/ppermute | solution.py:451
  11.6 34.8 %collective-permute-start.8 = (bf16[128,1536]{1,0:T(8,128)(2,1)S(1)}, bf16[128,1536]{1,0:T(8,128)(2,1)S(1)}, u32[]{:S(2)}, u32[]{:S(2)}) collective-permute-start(bf16[128,1536]{1,0:T(8,128)(2,1)S(1)} %second.1.refs_0_), channel_id=1, source_target_pairs={{0,2},{1,3},{2,0},{3,1},{4,6},{5,7},{6,4},{7,5},{8,10},{9,11},{10,... | collective-permute-start | bytes 1179656 | tf_op jit(solution)/shard_map/ppermute | solution.py:457
  37.8 16.3 %collective-permute-start.2 = (bf16[144,1536]{1,0:T(8,128)(2,1)}, bf16[144,1536]{1,0:T(8,128)(2,1)S(1)}, u32[]{:S(2)}, u32[]{:S(2)}) collective-permute-start(bf16[144,1536]{1,0:T(8,128)(2,1)} %collective-permute-done.1.refs_2_.refs_6_), channel_id=1, source_target_pairs={{0,1},{1,0},{2,3},{3,2},{4,5},{5,4},{6,7},{7,6},{8,9},{9,8},{10,11... | collective-permute-start | bytes 1327112 | tf_op jit(solution)/shard_map/ppermute | solution.py:457
  46.4 21.5 %collective-permute-start.9 = (bf16[128,1536]{1,0:T(8,128)(2,1)S(1)}, bf16[128,1536]{1,0:T(8,128)(2,1)S(1)}, u32[]{:S(2)}, u32[]{:S(2)}) collective-permute-start(bf16[128,1536]{1,0:T(8,128)(2,1)S(1)} %second.1.refs_0_), channel_id=1, source_target_pairs={{0,1},{1,0},{2,3},{3,2},{4,5},{5,4},{6,7},{7,6},{8,9},{9,8},{10,11... | collective-permute-start | bytes 1179656 | tf_op jit(solution)/shard_map/ppermute | solution.py:457
  47.0 20.9 %collective-permute-start.10 = (bf16[128,1536]{1,0:T(8,128)(2,1)S(1)}, bf16[128,1536]{1,0:T(8,128)(2,1)S(1)}, u32[]{:S(2)}, u32[]{:S(2)}) collective-permute-start(bf16[128,1536]{1,0:T(8,128)(2,1)S(1)} %collective-permute-done.8.refs_2_), channel_id=1, source_target_pairs={{0,1},{1,0},{2,3},{3,2},{4,5},{5,4},{6,7},{7,6},{8,9},{9,8},{10,11... | collective-permute-start | bytes 1179656 | tf_op jit(solution)/shard_map/ppermute | solution.py:457
  57.3 16.9 %collective-permute-start.5 = (bf16[256,1536]{1,0:T(8,128)(2,1)S(1)}, bf16[256,1536]{1,0:T(8,128)(2,1)S(1)}, u32[]{:S(2)}, u32[]{:S(2)}) collective-permute-start(bf16[256,1536]{1,0:T(8,128)(2,1)S(1)} %get-tuple-element.37), channel_id=1, source_target_pairs={{0,8},{4,12},{8,0},{12,4},{1,9},{5,13},{9,1},{13,5},{2,10},{6,14},... | collective-permute-start | bytes 2359304 | tf_op jit(solution)/shard_map/ppermute | solution.py:451
  70.7 16.5 %collective-permute-start.21 = (bf16[256,1536]{1,0:T(8,128)(2,1)S(1)}, bf16[256,1536]{1,0:T(8,128)(2,1)S(1)}, u32[]{:S(2)}, u32[]{:S(2)}) collective-permute-start(bf16[256,1536]{1,0:T(8,128)(2,1)S(1)} %get-tuple-element.50), channel_id=1, source_target_pairs={{0,8},{4,12},{8,0},{12,4},{1,9},{5,13},{9,1},{13,5},{2,10},{6,14},... | collective-permute-start | bytes 2359304 | tf_op jit(solution)/shard_map/ppermute | solution.py:451
  71.9 17.2 %collective-permute-start.6 = (bf16[128,1536]{1,0:T(8,128)(2,1)S(1)}, bf16[128,1536]{1,0:T(8,128)(2,1)S(1)}, u32[]{:S(2)}, u32[]{:S(2)}) collective-permute-start(bf16[128,1536]{1,0:T(8,128)(2,1)S(1)} %get-tuple-element.38), channel_id=1, source_target_pairs={{0,4},{4,0},{8,12},{12,8},{1,5},{5,1},{9,13},{13,9},{2,6},{6,2},{1... | collective-permute-start | bytes 1179656 | tf_op jit(solution)/shard_map/ppermute | solution.py:451
  72.0 15.4 %collective-permute-start.11 = (bf16[512,768]{1,0:T(8,128)(2,1)S(1)}, bf16[512,768]{1,0:T(8,128)(2,1)S(1)}, u32[]{:S(2)}, u32[]{:S(2)}) collective-permute-start(bf16[512,768]{1,0:T(8,128)(2,1)S(1)} %pad_maximum_fusion.1), channel_id=1, source_target_pairs={{0,4},{4,0},{8,12},{12,8},{1,5},{5,1},{9,13},{13,9},{2,6},{6,2},{1... | collective-permute-start | bytes 2359304 | tf_op jit(solution)/shard_map/ppermute | solution.py:451
  72.5 28.0 %collective-permute-start.15 = (bf16[768,768]{1,0:T(8,128)(2,1)S(1)}, bf16[768,768]{1,0:T(8,128)(2,1)S(1)}, u32[]{:S(2)}, u32[]{:S(2)}) collective-permute-start(bf16[768,768]{1,0:T(8,128)(2,1)S(1)} %slice.62), channel_id=1, source_target_pairs={{0,16},{16,0},{1,17},{17,1},{2,18},{18,2},{3,19},{19,3},{4,20},{20... | collective-permute-start | bytes 3538952 | tf_op jit(solution)/shard_map/ppermute | solution.py:454
  74.1 26.4 %collective-permute-start.14 = (bf16[1280,768]{1,0:T(8,128)(2,1)S(1)}, bf16[1280,768]{1,0:T(8,128)(2,1)S(1)}, u32[]{:S(2)}, u32[]{:S(2)}) collective-permute-start(bf16[1280,768]{1,0:T(8,128)(2,1)S(1)} %collective-permute-done.4.k_x.v_x.o_x), channel_id=1, source_target_pairs={{0,4},{4,0},{8,12},{12,8},{1,5},{5,1},{9,13},{13,9},{2,6},{6,2},{1... | collective-permute-start | bytes 5898248 | tf_op jit(solution)/shard_map/ppermute | solution.py:451
  87.3 7.5 %collective-permute-start.20 = (bf16[128,1536]{1,0:T(8,128)(2,1)S(1)}, bf16[128,1536]{1,0:T(8,128)(2,1)S(1)}, u32[]{:S(2)}, u32[]{:S(2)}) collective-permute-start(bf16[128,1536]{1,0:T(8,128)(2,1)S(1)} %get-tuple-element.49), channel_id=1, source_target_pairs={{0,4},{4,0},{8,12},{12,8},{1,5},{5,1},{9,13},{13,9},{2,6},{6,2},{1... | collective-permute-start | bytes 1179656 | tf_op jit(solution)/shard_map/ppermute | solution.py:451
  97.8 16.2 %collective-permute-start.13 = (bf16[128,2304]{1,0:T(8,128)(2,1)S(1)}, bf16[128,2304]{1,0:T(8,128)(2,1)S(1)}, u32[]{:S(2)}, u32[]{:S(2)}) collective-permute-start(bf16[128,2304]{1,0:T(8,128)(2,1)S(1)} %merge.2), channel_id=1, source_target_pairs={{0,8},{4,12},{8,0},{12,4},{1,9},{5,13},{9,1},{13,5},{2,10},{6,14},... | collective-permute-start | bytes 1769480 | tf_op jit(solution)/shard_map/ppermute | solution.py:451
  100.6 13.4 %collective-permute-start.16 = (bf16[768,768]{1,0:T(8,128)(2,1)S(1)}, bf16[768,768]{1,0:T(8,128)(2,1)S(1)}, u32[]{:S(2)}, u32[]{:S(2)}) collective-permute-start(bf16[768,768]{1,0:T(8,128)(2,1)S(1)} %collective-permute-done.15.o_y), channel_id=1, source_target_pairs={{0,4},{4,0},{8,12},{12,8},{1,5},{5,1},{9,13},{13,9},{2,6},{6,2},{1... | collective-permute-start | bytes 3538952 | tf_op jit(solution)/shard_map/ppermute | solution.py:451
  104.7 21.3 %collective-permute-start.24 = (bf16[128,2304]{1,0:T(8,128)(2,1)S(1)}, bf16[128,2304]{1,0:T(8,128)(2,1)S(1)}, u32[]{:S(2)}, u32[]{:S(2)}) collective-permute-start(bf16[128,2304]{1,0:T(8,128)(2,1)S(1)} %merge.3), channel_id=1, source_target_pairs={{0,8},{4,12},{8,0},{12,4},{1,9},{5,13},{9,1},{13,5},{2,10},{6,14},... | collective-permute-start | bytes 1769480 | tf_op jit(solution)/shard_map/ppermute | solution.py:451
  119.5 12.9 %collective-permute-start.18 = (bf16[128,1536]{1,0:T(8,128)(2,1)S(1)}, bf16[128,1536]{1,0:T(8,128)(2,1)S(1)}, u32[]{:S(2)}, u32[]{:S(2)}) collective-permute-start(bf16[128,1536]{1,0:T(8,128)(2,1)S(1)} %get-tuple-element.47), channel_id=1, source_target_pairs={{0,1},{1,0},{2,3},{3,2},{4,5},{5,4},{6,7},{7,6},{8,9},{9,8},{10,11... | collective-permute-start | bytes 1179656 | tf_op jit(solution)/shard_map/ppermute | solution.py:457
  120.3 43.0 %collective-permute-start.17 = (bf16[128,1536]{1,0:T(8,128)(2,1)S(1)}, bf16[128,1536]{1,0:T(8,128)(2,1)S(1)}, u32[]{:S(2)}, u32[]{:S(2)}) collective-permute-start(bf16[128,1536]{1,0:T(8,128)(2,1)S(1)} %get-tuple-element.46), channel_id=1, source_target_pairs={{0,1},{1,0},{2,3},{3,2},{4,5},{5,4},{6,7},{7,6},{8,9},{9,8},{10,11... | collective-permute-start | bytes 1179656 | tf_op jit(solution)/shard_map/ppermute | solution.py:457
  131.6 23.3 %collective-permute-start.25 = (bf16[128,1536]{1,0:T(8,128)(2,1)S(1)}, bf16[128,1536]{1,0:T(8,128)(2,1)S(1)}, u32[]{:S(2)}, u32[]{:S(2)}) collective-permute-start(bf16[128,1536]{1,0:T(8,128)(2,1)S(1)} %get-tuple-element.55), channel_id=1, source_target_pairs={{0,1},{1,0},{2,3},{3,2},{4,5},{5,4},{6,7},{7,6},{8,9},{9,8},{10,11... | collective-permute-start | bytes 1179656 | tf_op jit(solution)/shard_map/ppermute | solution.py:457
  132.5 30.8 %collective-permute-start.19 = (bf16[128,1536]{1,0:T(8,128)(2,1)S(1)}, bf16[128,1536]{1,0:T(8,128)(2,1)S(1)}, u32[]{:S(2)}, u32[]{:S(2)}) collective-permute-start(bf16[128,1536]{1,0:T(8,128)(2,1)S(1)} %fusion.5), channel_id=1, source_target_pairs={{0,2},{1,3},{2,0},{3,1},{4,6},{5,7},{6,4},{7,5},{8,10},{9,11},{10,... | collective-permute-start | bytes 1179656 | tf_op jit(solution)/shard_map/ppermute | solution.py:457
  155.0 21.2 %collective-permute-start.27 = (bf16[128,1536]{1,0:T(8,128)(2,1)S(1)}, bf16[128,1536]{1,0:T(8,128)(2,1)S(1)}, u32[]{:S(2)}, u32[]{:S(2)}) collective-permute-start(bf16[128,1536]{1,0:T(8,128)(2,1)S(1)} %fusion), channel_id=1, source_target_pairs={{0,2},{1,3},{2,0},{3,1},{4,6},{5,7},{6,4},{7,5},{8,10},{9,11},{10,... | collective-permute-start | bytes 1179656 | tf_op jit(solution)/shard_map/ppermute | solution.py:457
  159.2 17.0 %collective-permute-start.26 = (bf16[128,1536]{1,0:T(8,128)(2,1)S(1)}, bf16[128,1536]{1,0:T(8,128)(2,1)S(1)}, u32[]{:S(2)}, u32[]{:S(2)}) collective-permute-start(bf16[128,1536]{1,0:T(8,128)(2,1)S(1)} %get-tuple-element.56), channel_id=1, source_target_pairs={{0,1},{1,0},{2,3},{3,2},{4,5},{5,4},{6,7},{7,6},{8,9},{9,8},{10,11... | collective-permute-start | bytes 1179656 | tf_op jit(solution)/shard_map/ppermute | solution.py:457
  (17 other events, 191.9 us)
